TPU v7x, 512 devices: a whole 4x4x16 slice. The times are simulated.
512 devices in a mesh: rep: 64 (over y, z), fsdp: 8 (over x, core).
Axes of the slice: x: 4, y: 4, z: 16, core: 2. Of those that a mesh axis runs over, the one named last changes fastest.
Arguments:
- partial_grads: bfloat16 [64, 8, 64, 14336], P('rep', 'fsdp'), may hold values from -6 to 6
- momentum_old: float32 [64, 64, 14336], P('rep', None, 'fsdp'), may hold values from -6 to 6
- indices: int32 [64, 1, 224, 32], P('rep', None, 'fsdp'), may hold values from 0 to 4095, all different within a row
Outputs:
- new_momentum: float32 [64, 64, 14336], P('rep', None, 'fsdp')
- update: float32 [64, 14336], P(None, 'fsdp')
Inputs may be any that keep to these rules, and one draw needn't show every extreme that they name: `indices`: the 32 numbers of one replica's tile are distinct.
All inputs are finite; a program needn't handle non-finite values.
Results may differ from a plain program's by a relative error of at most 0.0003.
Values sent between devices are 32-bit elements; how exact they have to be, the bound alone decides.
No kernel may reach another device: no remote copies, remote signals or barrier semaphores. Data moves between devices by JAX's collectives and lax.ppermute only.
A program may use at most 64 MiB of HBM per device.

v0:
```python
import jax
import jax.numpy as jnp
from jax import lax
from jax.sharding import PartitionSpec as P

TILE = 64


BETA_DECAY = 0.999


def dct_cosines():
    counter = jnp.arange(TILE, dtype=jnp.float32)
    scales = jnp.where(counter == 0, jnp.sqrt(1.0 / TILE), jnp.sqrt(2.0 / TILE)).astype(jnp.float32)
    angles = jnp.pi * (counter[None, :] + 0.5) * counter[:, None] / TILE
    return scales[:, None] * jnp.cos(angles)


def forward(source, cosines):
    rows_count, cols_count = source.shape
    shaped = source.reshape(rows_count // TILE, TILE, cols_count // TILE, TILE)
    mixed = jnp.einsum("kn,anbm->akbm", cosines, shaped, precision=lax.Precision.HIGHEST)
    mixed = jnp.einsum("lm,akbm->akbl", cosines, mixed, precision=lax.Precision.HIGHEST)
    return mixed.reshape(rows_count, cols_count)


def inverse(source, cosines):
    rows_count, cols_count = source.shape
    shaped = source.reshape(rows_count // TILE, TILE, cols_count // TILE, TILE)
    mixed = jnp.einsum("kn,akbl->anbl", cosines, shaped, precision=lax.Precision.HIGHEST)
    mixed = jnp.einsum("lm,anbl->anbm", cosines, mixed, precision=lax.Precision.HIGHEST)
    return mixed.reshape(rows_count, cols_count)


def to_tiles(matrix):
    rows_count, cols_count = matrix.shape
    return matrix.reshape(rows_count // TILE, TILE, cols_count // TILE, TILE).transpose(0, 2, 1, 3)


def from_tiles(blocks):
    tile_rows, tile_cols = (blocks.shape[0], blocks.shape[1])
    return blocks.transpose(0, 2, 1, 3).reshape(tile_rows * TILE, tile_cols * TILE)


def hot_pair(numbers):
    counter = jnp.arange(TILE, dtype=jnp.int32)
    numbers = numbers.astype(jnp.int32)
    row_hot = ((numbers // TILE)[..., None] == counter).astype(jnp.float32)
    col_hot = ((numbers % TILE)[..., None] == counter).astype(jnp.float32)
    return (row_hot, col_hot)


def pick_own(coeff_matrix, numbers):
    blocks = to_tiles(coeff_matrix)
    row_hot, col_hot = hot_pair(numbers)
    along = jnp.einsum("abkm,abjm->abjk", blocks, col_hot, precision=lax.Precision.HIGHEST)
    selected = jnp.sum(along * row_hot, axis=-1)
    keep_mask = jnp.einsum("abjk,abjm->abkm", row_hot, col_hot, precision=lax.Precision.HIGHEST)
    own_dense = from_tiles(blocks * keep_mask)
    return (selected, own_dense)


def on_device(partial_grads, momentum_old, indices):
    cosines = dct_cosines()
    numbers = indices[0]
    gradient = lax.psum_scatter(
        partial_grads.astype(jnp.float32), "fsdp", scatter_dimension=3, tiled=True
    )
    momentum = BETA_DECAY * momentum_old[0] + gradient[0, 0]
    coeffs = forward(momentum, cosines)
    selected, own_dense = pick_own(coeffs, numbers)
    fresh = momentum - inverse(own_dense, cosines)
    sent_values = selected[None]
    sent_numbers = indices.astype(jnp.float32)
    values = lax.all_gather(sent_values, "rep", axis=0, tiled=True)
    sent = lax.all_gather(sent_numbers, "rep", axis=0, tiled=True)
    row_hot, col_hot = hot_pair(sent)
    weighted = values[..., None] * row_hot
    summed_tiles = jnp.einsum(
        "pabjk,pabjm->abkm", weighted, col_hot, precision=lax.Precision.HIGHEST
    )
    summed = from_tiles(summed_tiles)
    update = inverse(summed, cosines)
    return (fresh[None], update)


def solution(mesh):
    in_specs = (P("rep", "fsdp", None, None), P("rep", None, "fsdp"), P("rep", None, "fsdp", None))
    out_specs = (P("rep", None, "fsdp"), P(None, "fsdp"))
    return jax.shard_map(
        on_device, mesh=mesh, in_specs=in_specs, out_specs=out_specs, check_vma=False
    )
```

profile of v0, /device:TPU:4, one launch (start us, length us, event | category | flops | bytes accessed | tf_op | source)
XLA Modules:
  0.0 276.4 jit_solution(14265729670550805453)
XLA Ops:
  7.2 3.5 %convert_element_type.6 = f32[1,1,64,14336]{3,2,1,0:T(8,128)} convert(bf16[1,1,64,14336]{3,2,1,0:T(8,128)(2,1)} %param.3) | non-fusion elementwise | flops 917504 | bytes 5505024 | tf_op jit(solution)/shard_map/convert_element_type | solution.py:67
  10.8 0.7 convert_element_type.14
  11.5 1.1 broadcast_multiply_fusion
  12.6 0.4 mul.122
  13.0 107.5 %all_gather.6 = f32[64,1,28,32]{3,1,2,0:T(1,128)S(1)} all-gather(f32[1,1,28,32]{3,1,2,0:T(1,128)S(1)} %convert_element_type.14), channel_id=1, replica_groups=mesh['rep'=64,'fsdp'=8] {'rep'}, dimensions={0}, use_global_device_ids=true | all-gather | bytes 232960 | tf_op jit(solution)/shard_map/all_gather | solution.py:76
  120.5 0.8 copy.29
  121.4 0.7 add_select_fusion.3
  122.6 1.4 squeeze.10
  124.2 2.1 convolution_bitcast_fusion.3
  126.3 1.6 fusion.28
  127.9 1.0 fusion.11
  128.9 0.9 fusion.10
  129.9 1.6 convolution_bitcast_fusion.1
  131.5 1.6 fusion.25
  133.1 0.5 copy.28
  134.0 99.3 %all-gather.1 = f32[64,28,32]{2,1,0:T(8,128)S(1)} all-gather(f32[1,28,32]{2,1,0:T(8,128)S(1)} %bitcast.102), channel_id=2, replica_groups=mesh['rep'=64,'fsdp'=8] {'rep'}, dimensions={0}, use_global_device_ids=true | all-gather | bytes 232960 | tf_op jit(solution)/shard_map/all_gather | solution.py:75
  233.3 0.5 copy.30
  233.9 5.0 %fusion.67 = f32[64,28,32,64]{0,3,2,1:T(8,128)S(1)} fusion(f32[64,28,32]{0,2,1:T(8,128)S(1)} %copy.30, s32[64,28,32]{0,2,1:T(8,128)S(1)} %get-tuple-element.2), kind=kLoop, calls=%fused_computation.2.clone.clone.clone.2 | loop fusion | flops 7340032 | bytes 15138816 | tf_op jit(solution)/shard_map/pabjk,pabjm->abkm/dot_general | solution.py:79
  239.0 24.8 %fusion.6 = f32[64,28,64]{2,0,1:T(8,128)S(1)} fusion(s32[64,28,32]{0,2,1:T(8,128)S(1)} %get-tuple-element.3, f32[64,28,32,64]{0,3,2,1:T(8,128)S(1)} %fusion.67), kind=kOutput, calls=%fused_computation.12 | convolution fusion | flops 2822242304 | bytes 15368192 | tf_op jit(solution)/shard_map/pabjk,pabjm->abkm/dot_general | solution.py:79
  263.8 1.6 convolution_bitcast_fusion
  265.4 1.6 fusion.22
  267.1 0.5 copy.33
  267.6 1.1 reshape.193
  268.7 0.8 fusion.16
  (11 shorter events, 1.1 us)
Async XLA Ops:
  7.2 115.4 %reduce-scatter.2.cloned.1.call-start = ((), (), s32[]{:S(2)}) async-start(), calls=%async_computation.1 | async-start | bytes 4128768 | tf_op jit(solution)/shard_map/reduce_scatter | solution.py:66
  233.9 34.9 %copy-start = (f32[1,64,1792]{2,1,0:T(8,128)S(1)}, f32[1,64,1792]{2,1,0:T(8,128)}, u32[]{:S(2)}) copy-start(f32[1,64,1792]{2,1,0:T(8,128)} %param.4) | copy-start | bytes 1376260
  233.9 34.8 %copy-start.1 = (f32[1,1,64,1792]{3,2,1,0:T(8,128)S(1)}, f32[1,1,64,1792]{3,2,1,0:T(8,128)}, u32[]{:S(2)}) copy-start(f32[1,1,64,1792]{3,2,1,0:T(8,128)} %reduce-scatter.2.cloned.1.call-done) | copy-start | bytes 1376260
Sparse Core Ops, SparseCore 0:
  10.9 44.1 reduce-scatter.1
where the time goes:
time: 277 us; the launch traced here: 276 us
  blocking collectives  207 us (75%)
  matrix products  37 us (13%)
  between operations  14.2 us (5%)
  other arithmetic  12.6 us (5%)
  local copies, waits for them, and re-layouts  5.78 us (2%)
    all_gather x1, blocking collectives, on_device(): sent = lax.all_gather(sent_numbers, 'rep', axis=0, tiled=True)  108 us
    all_gather x1, blocking collectives, on_device(): values = lax.all_gather(sent_values, 'rep', axis=0, tiled=True)  99.3 us
    dot_general x1, matrix products, on_device(): jnp.einsum('pabjk,pabjm->abkm', weighted, col_hot, precision=lax.Precisio...  24.8 us
  transfers between devices with their start and end apart: 1, of which 0 were waited for; matrix products, arithmetic and copies ran while one was open for 2% of the time, Pallas kernels for 0%

commit v1 on v0

--- a/solution.py
+++ b/solution.py
@@ -60,6 +60,11 @@
     return (selected, own_dense)
 
 
+def gather_over_rep(block):
+    copies = jnp.broadcast_to(block, (64,) + block.shape[1:])
+    return lax.all_to_all(copies, "rep", 0, 0, tiled=True)
+
+
 def on_device(partial_grads, momentum_old, indices):
     cosines = dct_cosines()
     numbers = indices[0]
@@ -70,10 +75,10 @@
     coeffs = forward(momentum, cosines)
     selected, own_dense = pick_own(coeffs, numbers)
     fresh = momentum - inverse(own_dense, cosines)
-    sent_values = selected[None]
+    sent_values = selected
     sent_numbers = indices.astype(jnp.float32)
-    values = lax.all_gather(sent_values, "rep", axis=0, tiled=True)
-    sent = lax.all_gather(sent_numbers, "rep", axis=0, tiled=True)
+    values = gather_over_rep(sent_values[:, None])
+    sent = gather_over_rep(sent_numbers)
     row_hot, col_hot = hot_pair(sent)
     weighted = values[..., None] * row_hot
     summed_tiles = jnp.einsum(

time: 277 us -> 153 us (0.55)
  the two profiles are of different devices: /device:TPU:4 before, /device:TPU:7 now
where the time goes in v1:
time: 153 us; the launch traced here: 152 us
  matrix products  37.2 us (24%)
  starting transfers between devices  33.1 us (22%)
  waiting for transfers between devices  30.8 us (20%)
  other arithmetic  23.8 us (16%)
  between operations  14.2 us (9%)
  local copies, waits for them, and re-layouts  12.9 us (8%)
    all_to_all x2, starting transfers between devices, gather_over_rep(): return lax.all_to_all(copies, 'rep', 0, 0, tiled=True)  33 us
    all_to_all x2, waiting for transfers between devices, gather_over_rep(): return lax.all_to_all(copies, 'rep', 0, 0, tiled=True)  28.7 us
    dot_general x1, matrix products, on_device(): jnp.einsum('pabjk,pabjm->abkm', weighted, col_hot, precision=lax.Precisio...  25.1 us
    unnamed x8, local copies, waits for them, and re-layouts  6.76 us
    dot_general x1, other arithmetic, on_device(): jnp.einsum('pabjk,pabjm->abkm', weighted, col_hot, precision=lax.Precisio...  6.14 us
    unnamed x2, other arithmetic  5.84 us
    convert_element_type x1, other arithmetic, on_device(): partial_grads.astype(jnp.float32)  3.54 us
    dot_general x2, matrix products, inverse(): jnp.einsum('lm,anbl->anbm', cosines, mixed, precision=lax.Precision.HIGHEST)  3.27 us
  transfers between devices with their start and end apart: 3, of which 3 were waited for; matrix products, arithmetic and copies ran while one was open for 12% of the time, Pallas kernels for 0%

profile of v1, /device:TPU:7, one launch (start us, length us, event | category | flops | bytes accessed | tf_op | source)
XLA Modules:
  0.0 152.0 jit_solution(15854118216719854424)
XLA Ops:
  7.2 3.5 %convert_element_type.6 = f32[1,1,64,14336]{3,2,1,0:T(8,128)} convert(bf16[1,1,64,14336]{3,2,1,0:T(8,128)(2,1)} %param.3) | non-fusion elementwise | flops 917504 | bytes 5505024 | tf_op jit(solution)/shard_map/convert_element_type | solution.py:72
  12.6 2.9 %reduce.2 = f32[64,28,32]{2,1,0:T(8,128)S(1)} reduce(f32[64,28,1,32]{3,2,1,0:T(1,128)S(1)} %broadcast_bitcast_fusion.1, f32[]{:T(128)} %broadcast.184), dimensions={2}, to_apply=%broadcast_bitcast_fusion.1.reduce_sub_computation | reduce | bytes 458756
  15.5 1.1 reshape.201
  16.6 18.6 %all-to-all-start = ((f32[64,1,896]{2,1,0:T(1,128)}), f32[64,1,896]{2,1,0:T(1,128)S(1)}, u32[]{:S(2)}, u32[]{:S(2)}) async-start(f32[64,1,896]{2,1,0:T(1,128)} %reshape.201), calls=%async_computation.1 | async-start | bytes 458752 | tf_op jit(solution)/shard_map/all_to_all | solution.py:65
  37.5 15.2 %all-to-all-done = f32[64,1,896]{2,1,0:T(1,128)S(1)} async-done(((f32[64,1,896]{2,1,0:T(1,128)}), f32[64,1,896]{2,1,0:T(1,128)S(1)}, u32[]{:S(2)}, u32[]{:S(2)}) %all-to-all-start) | async-done | bytes 229408 | tf_op jit(solution)/shard_map/all_to_all | solution.py:65
  52.7 1.2 reduce.3
  53.9 1.5 %reshape.202 = f32[64,28,1,32]{3,2,1,0:T(1,128)S(1)} reshape(f32[64,896]{1,0:T(8,128)S(1)} %reduce.3) | data formatting | bytes 458752
  56.3 1.2 fusion.14
  57.5 2.2 %reduce-scatter.2.cloned.1.call-done = f32[1,1,64,1792]{3,2,1,0:T(8,128)} async-done(((f32[1,1,64,14336]{3,2,1,0:T(8,128)}), f32[1,1,64,1792]{3,2,1,0:T(8,128)}) %reduce-scatter.2.cloned.1.call-update) | async-done | bytes 458768 | tf_op jit(solution)/shard_map/reduce_scatter | solution.py:71
  59.6 1.4 squeeze.10
  61.3 2.1 %convolution_bitcast_fusion.3 = f32[64,28,64]{0,2,1:T(8,128)S(1)} fusion(f32[64,28,64]{2,1,0:T(8,128)S(1)} %add.58, f32[64]{0:T(128)S(1)} %get-tuple-element.7, f32[64]{0:T(128)S(1)} %get-tuple-element.6), kind=kOutput, calls=%fused_computation.11 | convolution fusion | flops 88092672 | bytes 918016 | tf_op jit(solution)/shard_map/kn,anbm->akbm/dot_general | solution.py:22
  63.3 1.6 %fusion.28 = f32[64,28,64]{2,0,1:T(8,128)S(1)} fusion(f32[64,28,64]{0,2,1:T(8,128)S(1)} %convolution_bitcast_fusion.3, f32[64]{0:T(128)S(1)} %get-tuple-element.7, f32[64]{0:T(128)S(1)} %get-tuple-element.6), kind=kOutput, calls=%fused_computation.44 | convolution fusion | flops 88092672 | bytes 918016 | tf_op jit(solution)/shard_map/lm,akbm->akbl/dot_general | solution.py:23
  67.4 2.9 %reduce.4 = f32[64,28,32]{2,1,0:T(8,128)S(1)} reduce(f32[64,28,1,32]{3,2,1,0:T(1,128)S(1)} %broadcast_bitcast_fusion, f32[]{:T(128)} %broadcast.184), dimensions={2}, to_apply=%broadcast_bitcast_fusion.reduce_sub_computation | reduce | bytes 458756
  71.4 14.4 %all-to-all-start.1 = ((f32[64,1,896]{2,1,0:T(1,128)}), f32[64,1,896]{2,1,0:T(1,128)S(1)}, u32[]{:S(2)}, u32[]{:S(2)}) async-start(f32[64,1,896]{2,1,0:T(1,128)} %reshape.203), calls=%async_computation.2 | async-start | bytes 458752 | tf_op jit(solution)/shard_map/all_to_all | solution.py:65
  85.8 1.6 %convolution_bitcast_fusion.1 = f32[64,28,64]{0,2,1:T(8,128)S(1)} fusion(f32[64,28,64]{2,0,1:T(8,128)S(1)} %fusion.10, f32[64]{0:T(128)S(1)} %get-tuple-element.7, f32[64]{0:T(128)S(1)} %get-tuple-element.6), kind=kOutput, calls=%fused_computation.9 | convolution fusion | flops 88092672 | bytes 918016 | tf_op jit(solution)/shard_map/kn,akbl->anbl/dot_general | solution.py:30
  87.4 1.6 %fusion.25 = f32[64,28,64]{2,0,1:T(8,128)S(1)} fusion(f32[64,28,64]{0,2,1:T(8,128)S(1)} %convolution_bitcast_fusion.1, f32[64]{0:T(128)S(1)} %get-tuple-element.7, f32[64]{0:T(128)S(1)} %get-tuple-element.6), kind=kOutput, calls=%fused_computation.41 | convolution fusion | flops 88092672 | bytes 918016 | tf_op jit(solution)/shard_map/lm,anbl->anbm/dot_general | solution.py:31
  90.0 2.0 %fusion.16 = f32[1,64,1792]{2,1,0:T(8,128)} fusion(f32[1,64,1792]{2,1,0:T(8,128)S(1)} %reshape.194, f32[1,1,64,1792]{3,2,1,0:T(8,128)} %reduce-scatter.2.cloned.1.call-done, f32[1,64,1792]{2,1,0:T(8,128)} %param.4), kind=kLoop, calls=%fused_computation.27 | loop fusion | flops 344064 | bytes 1835008 | tf_op jit(solution)/shard_map/sub | solution.py:77
  91.9 13.4 %all-to-all-done.1 = f32[64,1,896]{2,1,0:T(1,128)S(1)} async-done(((f32[64,1,896]{2,1,0:T(1,128)}), f32[64,1,896]{2,1,0:T(1,128)S(1)}, u32[]{:S(2)}, u32[]{:S(2)}) %all-to-all-start.1) | async-done | bytes 229408 | tf_op jit(solution)/shard_map/all_to_all | solution.py:65
  105.4 1.2 reduce.5
  106.5 1.5 %reshape.204 = f32[64,28,1,32]{3,2,1,0:T(1,128)S(1)} reshape(f32[64,896]{1,0:T(8,128)S(1)} %reduce.5) | data formatting | bytes 458752
  108.9 6.1 %fusion.67 = f32[64,28,32,64]{0,3,2,1:T(8,128)S(1)} fusion(f32[64,28,32]{0,2,1:T(8,128)S(1)} %bitcast.113, s32[64,28,32]{0,2,1:T(8,128)} %get-tuple-element.2), kind=kLoop, calls=%fused_computation.2.clone.clone.clone.2 | loop fusion | flops 7340032 | bytes 15138816 | tf_op jit(solution)/shard_map/pabjk,pabjm->abkm/dot_general | solution.py:84
  115.1 25.1 %fusion.6 = f32[64,28,64]{2,0,1:T(8,128)S(1)} fusion(s32[64,28,32]{0,2,1:T(8,128)S(1)} %get-tuple-element.3, f32[64,28,32,64]{0,3,2,1:T(8,128)S(1)} %fusion.67), kind=kOutput, calls=%fused_computation.12 | convolution fusion | flops 2822242304 | bytes 15368192 | tf_op jit(solution)/shard_map/pabjk,pabjm->abkm/dot_general | solution.py:84
  140.2 1.6 %convolution_bitcast_fusion = f32[64,28,64]{0,2,1:T(8,128)S(1)} fusion(f32[64,28,64]{2,0,1:T(8,128)S(1)} %fusion.6, f32[64]{0:T(128)S(1)} %get-tuple-element.7, f32[64]{0:T(128)S(1)} %get-tuple-element.6), kind=kOutput, calls=%fused_computation.8 | convolution fusion | flops 88092672 | bytes 918016 | tf_op jit(solution)/shard_map/kn,akbl->anbl/dot_general | solution.py:30
  141.8 1.6 %fusion.22 = f32[64,28,64]{2,0,1:T(8,128)S(1)} fusion(f32[64,28,64]{0,2,1:T(8,128)S(1)} %convolution_bitcast_fusion, f32[64]{0:T(128)S(1)} %get-tuple-element.7, f32[64]{0:T(128)S(1)} %get-tuple-element.6), kind=kOutput, calls=%fused_computation.38 | convolution fusion | flops 88092672 | bytes 918016 | tf_op jit(solution)/shard_map/lm,anbl->anbm/dot_general | solution.py:31
  (21 shorter events, 12.0 us)
Async XLA Ops:
  7.2 52.5 %reduce-scatter.2.cloned.1.call-start = ((), (), s32[]{:S(2)}) async-start(), calls=%async_computation.3 | async-start | bytes 4128768 | tf_op jit(solution)/shard_map/reduce_scatter | solution.py:71
  16.6 36.1 %all-to-all-start = ((f32[64,1,896]{2,1,0:T(1,128)}), f32[64,1,896]{2,1,0:T(1,128)S(1)}, u32[]{:S(2)}, u32[]{:S(2)}) async-start(f32[64,1,896]{2,1,0:T(1,128)} %reshape.201), calls=%async_computation.1 | async-start | bytes 458752 | tf_op jit(solution)/shard_map/all_to_all | solution.py:65
  71.4 34.0 %all-to-all-start.1 = ((f32[64,1,896]{2,1,0:T(1,128)}), f32[64,1,896]{2,1,0:T(1,128)S(1)}, u32[]{:S(2)}, u32[]{:S(2)}) async-start(f32[64,1,896]{2,1,0:T(1,128)} %reshape.203), calls=%async_computation.2 | async-start | bytes 458752 | tf_op jit(solution)/shard_map/all_to_all | solution.py:65
Sparse Core Ops, SparseCore 0:
  10.9 48.6 reduce-scatter.1

commit v2 on v0

v2 whole, which is shorter than its diff:
```python
import functools

import jax
import jax.numpy as jnp
import ml_dtypes
import numpy as np
from jax import lax
from jax.experimental import pallas as pl
from jax.experimental.pallas import tpu as pltpu
from jax.sharding import PartitionSpec as P

TILE = 64
KEPT = 32
LANES = 128
GROUP = LANES // KEPT
WIDE = GROUP * TILE
BETA_DECAY = 0.999
F32 = jnp.float32
BF16 = jnp.bfloat16


def split_table(table):
    high = table.astype(ml_dtypes.bfloat16)
    low = (table - high.astype(np.float64)).astype(ml_dtypes.bfloat16)
    return high, low


def dct_cosines():
    counter = np.arange(TILE)
    scales = np.where(counter == 0, np.sqrt(1.0 / TILE), np.sqrt(2.0 / TILE))
    return scales[:, None] * np.cos(np.pi * (counter[None, :] + 0.5) * counter[:, None] / TILE)


def pick_table():
    high, low = split_table(dct_cosines().T)
    zero = np.zeros_like(high)
    return np.block([[high, zero], [low, zero], [zero, high], [zero, low]])


def wide_table():
    high, low = split_table(dct_cosines())
    eye = np.eye(GROUP)
    return np.concatenate([np.kron(eye, high.astype(np.float32)), np.kron(eye, low.astype(np.float32))], 0).astype(
        ml_dtypes.bfloat16
    )


def tall_table():
    high, low = split_table(dct_cosines().T)
    return np.concatenate([high, low, high], 1)


def halves(value):
    high = value.astype(BF16)
    return high, (value - high.astype(F32)).astype(BF16)


def cosine_rows(table, row):
    counter = lax.broadcasted_iota(jnp.int32, (TILE, LANES), 0)
    hot = jnp.concatenate([counter == (row >> 6), counter == (row & 63)], 0)
    both = jnp.dot(table, jnp.where(hot, 1.0, 0.0).astype(BF16), preferred_element_type=F32)
    down = both[:TILE] + both[TILE : 2 * TILE]
    own = (lax.broadcasted_iota(jnp.int32, (WIDE, LANES), 0) // TILE) == (
        lax.broadcasted_iota(jnp.int32, (WIDE, LANES), 1) // KEPT
    )
    high = jnp.concatenate([both[2 * TILE : 3 * TILE]] * GROUP, 0)
    low = jnp.concatenate([both[3 * TILE :]] * GROUP, 0)
    high = jnp.where(own, high, 0.0).astype(BF16)
    low = jnp.where(own, low, 0.0).astype(BF16)
    return down, jnp.concatenate([high, low], 1)


def picked(source, down, across):
    mixed = jnp.dot(source, across, preferred_element_type=F32)
    return jnp.sum((mixed[:, :LANES] + mixed[:, LANES:]) * down, axis=0, keepdims=True)


def pick_kernel(table_ref, grads_ref, numbers_ref, momentum_ref, own_numbers_ref, values_ref, wide_ref, own_ref):
    groups = numbers_ref.shape[1]
    wide_ref[0] = grads_ref[...].astype(F32)
    for group in range(groups):
        columns = slice(group * WIDE, (group + 1) * WIDE)
        down, across = cosine_rows(table_ref[...], numbers_ref[0, group : group + 1, :])
        values_ref[0, group : group + 1, :] = picked(grads_ref[:, columns], down, across)

    @pl.when(pl.program_id(0) == 0)
    def _():
        for group in range(groups):
            columns = slice(group * WIDE, (group + 1) * WIDE)
            down, across = cosine_rows(table_ref[...], own_numbers_ref[group : group + 1, :])
            high, low = halves(momentum_ref[:, columns])
            own_ref[group : group + 1, :] = BETA_DECAY * (picked(high, down, across) + picked(low, down, across))


def pick(grads, numbers, momentum, own_numbers):
    parts, groups, _ = numbers.shape
    rows, columns = momentum.shape
    return pl.pallas_call(
        pick_kernel,
        grid=(parts,),
        in_specs=[
            pl.BlockSpec((4 * TILE, LANES), lambda i: (0, 0)),
            pl.BlockSpec((rows, columns), lambda i: (0, i)),
            pl.BlockSpec((1, groups, LANES), lambda i: (i, 0, 0)),
            pl.BlockSpec((rows, columns), lambda i: (0, 0)),
            pl.BlockSpec((groups, LANES), lambda i: (0, 0)),
        ],
        out_specs=[
            pl.BlockSpec((1, groups, LANES), lambda i: (i, 0, 0)),
            pl.BlockSpec((1, rows, columns), lambda i: (i, 0, 0)),
            pl.BlockSpec((groups, LANES), lambda i: (0, 0)),
        ],
        out_shape=[
            jax.ShapeDtypeStruct((parts, groups, LANES), F32),
            jax.ShapeDtypeStruct((parts, rows, columns), F32),
            jax.ShapeDtypeStruct((groups, LANES), F32),
        ],
        compiler_params=pltpu.CompilerParams(vmem_limit_bytes=32 * 2**20),
        name="pick",
    )(jnp.asarray(pick_table()), grads, numbers, momentum, own_numbers)


def parts_of(numbers, values):
    numbers = numbers.astype(jnp.int32)
    lane_tile = lax.broadcasted_iota(jnp.int32, numbers.shape, numbers.ndim - 1) // KEPT
    high = values.astype(BF16).astype(F32)
    return (numbers >> 6).astype(F32), ((numbers & 63) + lane_tile * TILE).astype(F32), high, values - high


def hot_rows(row, column, high, low):
    def spread(value, count):
        return jnp.broadcast_to(value, (count, LANES)).astype(BF16)

    counter = lax.broadcasted_iota(jnp.int32, (WIDE, LANES), 0).astype(F32).astype(BF16)
    zero = jnp.zeros((), BF16)
    at_row = counter[:TILE] == spread(row, TILE)
    at_column = counter == spread(column, WIDE)
    weighted = jnp.concatenate(
        [jnp.where(at_row, spread(high, TILE), zero), jnp.where(at_row, spread(low, TILE), zero)], 0
    )
    return weighted, jnp.where(at_column, jnp.ones((), BF16), zero)


NT = (((1,), (1,)), ((), ()))


def back(dense, tall, wide):
    high, low = halves(dense)
    half = jnp.dot(tall, jnp.concatenate([high, high, low], 0), preferred_element_type=F32)
    high, low = halves(half)
    both = jnp.dot(jnp.concatenate([high, low], 0), wide[:WIDE], preferred_element_type=F32)
    return both[:TILE] + both[TILE:] + jnp.dot(high, wide[WIDE:], preferred_element_type=F32)


def spread_kernel(
    tall_ref, wide_ref, sent_ref, own_ref, momentum_ref, grad_ref, fresh_ref, update_ref, rows_ref, left_ref, right_ref
):
    replicas = sent_ref.shape[0]
    groups = momentum_ref.shape[1] // WIDE
    batch = left_ref.shape[2] // LANES
    step = 8
    values = sent_ref[:, :8, :]
    numbers = sent_ref[:, 8:, :]
    for part, value in enumerate(parts_of(numbers, values)):
        rows_ref[part] = value

    for group in range(groups):
        columns = slice(group * WIDE, (group + 1) * WIDE)
        total = jnp.zeros((2 * TILE, WIDE), F32)
        for first in range(0, replicas, batch):
            slot = (first // batch) % 2
            for replica in range(batch):
                lanes = slice(replica * LANES, (replica + 1) * LANES)
                left, right = hot_rows(*(rows_ref[part, first + replica, group : group + 1, :] for part in range(4)))
                left_ref[slot, :, lanes] = left
                right_ref[slot, :, lanes] = right
            total += lax.dot_general(left_ref[slot], right_ref[slot], NT, preferred_element_type=F32)
        update_ref[:, columns] = back(total[:TILE] + total[TILE:], tall_ref[...], wide_ref[...])

        own = parts_of(own_ref[8 + group : 9 + group, :], own_ref[group : group + 1, :])
        left, right = hot_rows(*own)
        dense = lax.dot_general(left, right, NT, preferred_element_type=F32)
        shared = back(dense[:TILE] + dense[TILE:], tall_ref[...], wide_ref[...])
        fresh_ref[:, columns] = BETA_DECAY * momentum_ref[:, columns] + grad_ref[:, columns] - shared


def spread(sent, own, momentum, grad, batch=8):
    rows, columns = momentum.shape
    replicas = sent.shape[0]
    return pl.pallas_call(
        spread_kernel,
        out_shape=[jax.ShapeDtypeStruct((rows, columns), F32)] * 2,
        scratch_shapes=[
            pltpu.VMEM((4, replicas, 8, LANES), F32),
            pltpu.VMEM((2, 2 * TILE, batch * LANES), BF16),
            pltpu.VMEM((2, WIDE, batch * LANES), BF16),
        ],
        compiler_params=pltpu.CompilerParams(vmem_limit_bytes=32 * 2**20),
        name="spread",
    )(jnp.asarray(tall_table()), jnp.asarray(wide_table()), sent, own, momentum, grad)


FSDP = ("x", "core")


def copies_to(block, count, axis):
    return lax.all_to_all(jnp.broadcast_to(block[None], (count,) + block.shape), axis, 0, 0, tiled=True)


def on_device(partial_grads, momentum_old, indices):
    groups = indices.shape[2] // GROUP
    momentum = momentum_old[0]
    own_numbers = indices.reshape(groups, LANES)
    parts = lax.axis_size(FSDP)
    numbers = copies_to(own_numbers, parts, FSDP)
    values, wide, own_part = pick(partial_grads[0, 0], numbers, momentum, own_numbers)
    grad = lax.psum_scatter(wide, FSDP, scatter_dimension=0, tiled=True)[0]
    values = lax.all_to_all(values, FSDP, 0, 0, tiled=True)
    selected = jnp.sum(values, axis=0) + own_part
    own = jnp.concatenate(
        [jnp.pad(part, ((0, 8 - groups), (0, 0))) for part in (selected, own_numbers.astype(F32))], 0
    )
    sent = copies_to(own, lax.axis_size("z"), "z")
    sent = copies_to(sent, lax.axis_size("y"), "y").reshape(-1, 16, LANES)
    fresh, update = spread(sent, own, momentum, grad)
    return fresh[None], update


def solution(mesh):
    fine = jax.sharding.Mesh(mesh.devices.reshape(4, 16, 4, 2), ("y", "z", "x", "core"))
    rep = ("y", "z")
    in_specs = (P(rep, FSDP, None, None), P(rep, None, FSDP), P(rep, None, FSDP, None))
    out_specs = (P(rep, None, FSDP), P(None, FSDP))
    return jax.shard_map(on_device, mesh=fine, in_specs=in_specs, out_specs=out_specs, check_vma=False)
```

time: 277 us -> 108 us (0.39)
  the two profiles are of different devices: /device:TPU:4 before, /device:TPU:32 now
where the time goes in v2:
time: 108 us; the launch traced here: 107 us
  blocking collectives  50.9 us (47%)
  Pallas kernels  26.4 us (24%)
  between operations  14.1 us (13%)
  local copies, waits for them, and re-layouts  6.29 us (6%)
  waiting for transfers between devices  5.37 us (5%)
  starting transfers between devices  3.39 us (3%)
    all_to_all x3, blocking collectives, copies_to(): lax.all_to_all(jnp.broadcast_to(block[None], (count,) + block.shape), axi...  50.9 us
    pallas_call x1, Pallas kernels, spread(): pl.pallas_call(spread_kernel, out_shape=[jax.ShapeDtypeStruct((rows, colu...  19.3 us
    pallas_call x1, Pallas kernels, pick(): pl.pallas_call(pick_kernel, grid=(parts,), in_specs=[pl.BlockSpec((4 * TI...  7.08 us
    unnamed x16, local copies, waits for them, and re-layouts  6.17 us
    all_to_all x1, waiting for transfers between devices, on_device(): values = lax.all_to_all(values, FSDP, 0, 0, tiled=True)  5.35 us
    all_to_all x1, starting transfers between devices, on_device(): values = lax.all_to_all(values, FSDP, 0, 0, tiled=True)  3.35 us
  transfers between devices with their start and end apart: 2, of which 1 were waited for; matrix products, arithmetic and copies ran while one was open for 0% of the time, Pallas kernels for 0%

profile of v2, /device:TPU:32, one launch (start us, length us, event | category | flops | bytes accessed | tf_op | source)
XLA Modules:
  0.0 107.3 jit_solution(3955373627094436228)
XLA Ops:
  7.2 0.0 reduce-scatter.2.cloned.1.call-start
  7.2 0.8 reduce
  8.0 0.1 broadcast_in_dim.10.own_numbers_ref
  8.0 9.5 %all_to_all.20.numbers_ref = s32[8,7,128]{2,1,0:T(8,128)S(1)} all-to-all(s32[8,7,128]{2,1,0:T(8,128)S(1)} %broadcast_in_dim.11), channel_id=1, replica_groups=mesh['y'=4,'z'=16,'x'=4,'core'=2] {'x','core'}, dimensions={0} | all-to-all | bytes 57344 | tf_op jit(solution)/shard_map/all_to_all | solution.py:207
  17.6 0.0 copy-start.1
  17.6 1.5 %copy-done.1 = bf16[1,1,64,14336]{3,2,1,0:T(8,128)(2,1)S(1)} copy-done((bf16[1,1,64,14336]{3,2,1,0:T(8,128)(2,1)S(1)}, bf16[1,1,64,14336]{3,2,1,0:T(8,128)(2,1)}, u32[]{:S(2)}) %copy-start.1) | copy-done | bytes 1835032
  19.1 0.0 copy-start.2
  19.1 1.0 copy-done.2
  20.1 0.8 copy-done.6
  20.9 0.0 copy-start.5
  20.9 0.0 copy-start.7
  20.9 7.1 %pick.1 = (f32[8,7,128]{2,1,0:T(8,128)}, f32[8,64,1792]{2,1,0:T(8,128)S(1)}, f32[7,128]{1,0:T(8,128)S(1)}) custom-call(bf16[256,128]{1,0:T(8,128)(2,1)S(1)} %copy-done.6, bf16[64,14336]{1,0:T(8,128)(2,1)S(1)} %bitcast.6, s32[8,7,128]{2,1,0:T(8,128)S(1)} %all_to_all.20.numbers_ref, f32[64,1792]{1,0:T(8,128)S(1)} %bitcast.7, ...), custom_call_target="tpu_custom_call" | custom-call | tf_op jit(solution)/shard_map/pick/pallas_call | solution.py:98
  28.0 1.8 %copy-done = f32[8,64,1792]{2,1,0:T(8,128)} copy-done((f32[8,64,1792]{2,1,0:T(8,128)}, f32[8,64,1792]{2,1,0:T(8,128)S(1)}, u32[]{:S(2)}) %copy-start) | copy-done | bytes 3670040
  29.8 0.0 reduce-scatter.2.cloned.1.call-update
  29.8 3.4 %all-to-all-start.1 = ((f32[8,7,128]{2,1,0:T(8,128)}), f32[8,7,128]{2,1,0:T(8,128)S(1)}, u32[]{:S(2)}, u32[]{:S(2)}) async-start(f32[8,7,128]{2,1,0:T(8,128)} %get-tuple-element.7), calls=%async_computation.1 | async-start | bytes 65536 | tf_op jit(solution)/shard_map/all_to_all | solution.py:218
  33.2 5.4 %all-to-all-done.1 = f32[8,7,128]{2,1,0:T(8,128)S(1)} async-done(((f32[8,7,128]{2,1,0:T(8,128)}), f32[8,7,128]{2,1,0:T(8,128)S(1)}, u32[]{:S(2)}, u32[]{:S(2)}) %all-to-all-start.1) | async-done | bytes 28704 | tf_op jit(solution)/shard_map/all_to_all | solution.py:218
  38.6 29.1 %all_to_all.21 = f32[16,16,128]{2,1,0:T(8,128)S(1)} all-to-all(f32[16,16,128]{2,1,0:T(8,128)S(1)} %broadcast_in_dim.24), channel_id=1, replica_groups=mesh['y'=4,'z'=16,'x'=4,'core'=2] {'z'}, dimensions={0} | all-to-all | bytes 262144 | tf_op jit(solution)/shard_map/all_to_all | solution.py:207
  67.7 12.3 %all_to_all.22 = f32[4,16,16,128]{3,2,1,0:T(8,128)S(1)} all-to-all(f32[4,16,16,128]{3,2,1,0:T(8,128)S(1)} %broadcast_in_dim.25), channel_id=1, replica_groups=mesh['y'=4,'z'=16,'x'=4,'core'=2] {'y'}, dimensions={0} | all-to-all | bytes 1048576 | tf_op jit(solution)/shard_map/all_to_all | solution.py:207
  80.1 0.0 copy-done.3
  80.1 0.0 copy-done.5
  80.1 0.0 copy-done.7
  80.1 0.0 copy-start.4
  80.1 1.0 copy-done.4
  81.1 19.3 %spread.1 = (f32[64,1792]{1,0:T(8,128)}, f32[64,1792]{1,0:T(8,128)}) custom-call(bf16[64,192]{1,0:T(8,128)(2,1)S(1)} %copy-done.7, bf16[512,256]{1,0:T(8,128)(2,1)S(1)} %copy-done.5, f32[64,16,128]{2,1,0:T(8,128)S(1)} %bitcast.5, f32[16,128]{1,0:T(8,128)S(1)} %select_maximum_fusion.own_ref, f32[64,1792]{1,0:T(8,128)S(1)} %bitcast.8, f32[64,1792]{1,0:T(8,128)S(1)} %bitcast.9), custom_call_target="tpu_custom_call" | custom-call | tf_op jit(solution)/shard_map/spread/pallas_call | solution.py:190
  (11 shorter events, 0.1 us)
Async XLA Ops:
  7.2 72.9 %reduce-scatter.2.cloned.1.call-start = ((), (), s32[]{:S(2)}) async-start(), calls=%async_computation.5 | async-start | bytes 4128768 | tf_op jit(solution)/shard_map/reduce_scatter | solution.py:217
  17.6 1.5 %copy-start.1 = (bf16[1,1,64,14336]{3,2,1,0:T(8,128)(2,1)S(1)}, bf16[1,1,64,14336]{3,2,1,0:T(8,128)(2,1)}, u32[]{:S(2)}) copy-start(bf16[1,1,64,14336]{3,2,1,0:T(8,128)(2,1)} %param.6) | copy-start | bytes 5505028
  19.1 1.0 copy-start.2
  20.1 0.8 copy-start.6
  20.9 59.1 %copy-start.3 = (f32[1,64,1792]{2,1,0:T(8,128)S(1)}, f32[1,64,1792]{2,1,0:T(8,128)}, u32[]{:S(2)}) copy-start(f32[1,64,1792]{2,1,0:T(8,128)} %param.7) | copy-start | bytes 1376260
  20.9 59.1 %copy-start.5 = (bf16[512,256]{1,0:T(8,128)(2,1)S(1)}, bf16[512,256]{1,0:T(8,128)(2,1)}, u32[]{:S(2)}) copy-start(bf16[512,256]{1,0:T(8,128)(2,1)} %constant.12.clone.wide_ref) | copy-start | bytes 786436
  20.9 59.1 %copy-start.7 = (bf16[64,192]{1,0:T(8,128)(2,1)S(1)}, bf16[64,192]{1,0:T(8,128)(2,1)}, u32[]{:S(2)}) copy-start(bf16[64,192]{1,0:T(8,128)(2,1)} %constant.11.clone.tall_ref) | copy-start | bytes 73732
  28.0 1.8 %copy-start = (f32[8,64,1792]{2,1,0:T(8,128)}, f32[8,64,1792]{2,1,0:T(8,128)S(1)}, u32[]{:S(2)}) copy-start(f32[8,64,1792]{2,1,0:T(8,128)S(1)} %get-tuple-element.9) | copy-start | bytes 11010052
  29.8 8.7 %all-to-all-start.1 = ((f32[8,7,128]{2,1,0:T(8,128)}), f32[8,7,128]{2,1,0:T(8,128)S(1)}, u32[]{:S(2)}, u32[]{:S(2)}) async-start(f32[8,7,128]{2,1,0:T(8,128)} %get-tuple-element.7), calls=%async_computation.1 | async-start | bytes 65536 | tf_op jit(solution)/shard_map/all_to_all | solution.py:218
  80.1 1.0 copy-start.4
Sparse Core Ops, SparseCore 0:
  30.0 46.8 reduce-scatter.1

commit v3 on v2

v3 whole, which is shorter than its diff:
```python
import functools

import jax
import jax.numpy as jnp
import ml_dtypes
import numpy as np
from jax import lax
from jax.experimental import pallas as pl
from jax.experimental.pallas import tpu as pltpu
from jax.sharding import PartitionSpec as P

TILE = 64
KEPT = 32
LANES = 128
GROUP = LANES // KEPT
WIDE = GROUP * TILE
BETA_DECAY = 0.999
WHOLE_VMEM = 60 * 2**20
F32 = jnp.float32
BF16 = jnp.bfloat16


def split_table(table):
    high = table.astype(ml_dtypes.bfloat16)
    low = (table - high.astype(np.float64)).astype(ml_dtypes.bfloat16)
    return high, low


def dct_cosines():
    counter = np.arange(TILE)
    scales = np.where(counter == 0, np.sqrt(1.0 / TILE), np.sqrt(2.0 / TILE))
    return scales[:, None] * np.cos(np.pi * (counter[None, :] + 0.5) * counter[:, None] / TILE)


def pick_table():
    high, low = split_table(dct_cosines().T)
    zero = np.zeros_like(high)
    return np.block([[high, zero], [low, zero], [zero, high], [zero, low]])


def wide_table():
    high, low = split_table(dct_cosines())
    eye = np.eye(GROUP)
    return np.concatenate([np.kron(eye, high.astype(np.float32)), np.kron(eye, low.astype(np.float32))], 0).astype(
        ml_dtypes.bfloat16
    )


def tall_table():
    high, low = split_table(dct_cosines().T)
    return np.concatenate([high, low, high], 1)


def halves(value):
    high = value.astype(BF16)
    return high, (value - high.astype(F32)).astype(BF16)


def cosine_rows(table, row):
    counter = lax.broadcasted_iota(jnp.int32, (TILE, LANES), 0)
    hot = jnp.concatenate([counter == (row >> 6), counter == (row & 63)], 0)
    both = jnp.dot(table, jnp.where(hot, 1.0, 0.0).astype(BF16), preferred_element_type=F32)
    down = both[:TILE] + both[TILE : 2 * TILE]
    own = (lax.broadcasted_iota(jnp.int32, (WIDE, LANES), 0) // TILE) == (
        lax.broadcasted_iota(jnp.int32, (WIDE, LANES), 1) // KEPT
    )
    high = jnp.concatenate([both[2 * TILE : 3 * TILE]] * GROUP, 0)
    low = jnp.concatenate([both[3 * TILE :]] * GROUP, 0)
    high = jnp.where(own, high, 0.0).astype(BF16)
    low = jnp.where(own, low, 0.0).astype(BF16)
    return down, jnp.concatenate([high, low], 1)


def picked(source, down, across):
    mixed = jnp.dot(source, across, preferred_element_type=F32)
    return jnp.sum((mixed[:, :LANES] + mixed[:, LANES:]) * down, axis=0, keepdims=True)


def pick_kernel(table_ref, grads_ref, numbers_ref, values_ref):
    groups = numbers_ref.shape[1]
    for group in range(groups):
        columns = slice(group * WIDE, (group + 1) * WIDE)
        down, across = cosine_rows(table_ref[...], numbers_ref[0, group : group + 1, :])
        values_ref[0, group : group + 1, :] = picked(grads_ref[:, columns], down, across)


def own_kernel(table_ref, momentum_ref, numbers_ref, own_ref):
    for group in range(numbers_ref.shape[0]):
        columns = slice(group * WIDE, (group + 1) * WIDE)
        down, across = cosine_rows(table_ref[...], numbers_ref[group : group + 1, :])
        high, low = halves(momentum_ref[:, columns])
        own_ref[group : group + 1, :] = BETA_DECAY * (picked(high, down, across) + picked(low, down, across))


def pick_own(momentum, numbers):
    return pl.pallas_call(
        own_kernel,
        out_shape=jax.ShapeDtypeStruct(numbers.shape, F32),
        cost_estimate=pl.CostEstimate(flops=4 * 10**8, bytes_accessed=2**19, transcendentals=0),
        compiler_params=pltpu.CompilerParams(vmem_limit_bytes=32 * 2**20),
        name="pick_own",
    )(jnp.asarray(pick_table()), momentum, numbers)


def pick(grads, numbers):
    parts, groups, _ = numbers.shape
    rows, columns = grads.shape
    return pl.pallas_call(
        pick_kernel,
        grid=(parts,),
        in_specs=[
            pl.BlockSpec((4 * TILE, LANES), lambda i: (0, 0)),
            pl.BlockSpec((rows, columns // parts), lambda i: (0, i)),
            pl.BlockSpec((1, groups, LANES), lambda i: (i, 0, 0)),
        ],
        out_specs=pl.BlockSpec((1, groups, LANES), lambda i: (i, 0, 0)),
        out_shape=jax.ShapeDtypeStruct((parts, groups, LANES), F32),
        cost_estimate=pl.CostEstimate(flops=2 * 10**9, bytes_accessed=2**21, transcendentals=0),
        compiler_params=pltpu.CompilerParams(vmem_limit_bytes=WHOLE_VMEM),
        name="pick",
    )(jnp.asarray(pick_table()), grads, numbers)


def parts_of(numbers, values):
    numbers = numbers.astype(jnp.int32)
    high = values.astype(BF16).astype(F32)
    return (numbers >> 6).astype(F32), (numbers & 63).astype(F32), high, values - high


SLAB = 16


def one_hots(row, column, high, low):
    row, column, high, low = (jnp.broadcast_to(part, (SLAB, LANES)).astype(BF16) for part in (row, column, high, low))
    counter = lax.broadcasted_iota(jnp.int32, (SLAB, LANES), 0).astype(F32).astype(BF16)
    counters = [counter + jnp.asarray(first, BF16) for first in range(0, TILE, SLAB)]
    zero, one = jnp.zeros((SLAB, LANES), BF16), jnp.ones((SLAB, LANES), BF16)
    at_row = [row == counter for counter in counters]
    weighted = [jnp.where(at, part, zero) for part in (high, low) for at in at_row]
    return jnp.concatenate(weighted, 0), jnp.concatenate([jnp.where(column == at, one, zero) for at in counters], 0)


NT = (((1,), (1,)), ((), ()))


def back(dense, tall, wide):
    high, low = halves(dense)
    half = jnp.dot(tall, jnp.concatenate([high, high, low], 0), preferred_element_type=F32)
    high, low = halves(half)
    both = jnp.dot(jnp.concatenate([high, low], 0), wide[:WIDE], preferred_element_type=F32)
    return both[:TILE] + both[TILE:] + jnp.dot(high, wide[WIDE:], preferred_element_type=F32)


def by_tile(block):
    lane_part = lax.broadcasted_iota(jnp.int32, (SLAB, LANES), 1) // KEPT
    rows = [block[SLAB * part : SLAB * (part + 1)] for part in range(GROUP)]
    tiles = []
    for tile in range(GROUP):
        moved = [pltpu.roll(rows[p], (KEPT * (p - tile)) % LANES, 1) if p != tile else rows[p] for p in range(GROUP)]
        total = moved[0]
        for part in range(1, GROUP):
            total = jnp.where(lane_part == part, moved[part], total)
        tiles.append(total)
    return tiles


def scattered(rows_ref, count):
    made = [one_hots(*(rows_ref[part, row : row + 1, :] for part in range(4))) for row in range(count)]
    total = lax.dot_general(
        jnp.concatenate([left for left, _ in made], 1),
        jnp.concatenate([right for _, right in made], 1),
        NT,
        preferred_element_type=F32,
    )
    return total[:TILE] + total[TILE:]


def spread_kernel(tall_ref, wide_ref, sent_ref, update_ref, rows_ref):
    groups = update_ref.shape[1] // WIDE
    replicas = sent_ref.shape[0] // SLAB
    for group in range(groups):
        values = by_tile(sent_ref[pl.ds(group, replicas, stride=SLAB), :])
        numbers = by_tile(sent_ref[pl.ds(SLAB // 2 + group, replicas, stride=SLAB), :])
        for tile in range(GROUP):
            for part, value in enumerate(parts_of(numbers[tile], values[tile])):
                rows_ref[group % 2, tile, part] = value
        dense = [scattered(rows_ref.at[group % 2, tile], SLAB) for tile in range(GROUP)]
        update_ref[:, group * WIDE : (group + 1) * WIDE] = back(
            jnp.concatenate(dense, 1), tall_ref[...], wide_ref[...]
        )


def spread(sent, columns):
    return pl.pallas_call(
        spread_kernel,
        out_shape=jax.ShapeDtypeStruct((TILE, columns), F32),
        scratch_shapes=[pltpu.VMEM((2, GROUP, 4, SLAB, LANES), F32)],
        compiler_params=pltpu.CompilerParams(vmem_limit_bytes=32 * 2**20),
        cost_estimate=pl.CostEstimate(flops=2 * 10**9, bytes_accessed=2**20, transcendentals=0),
        name="spread",
    )(jnp.asarray(tall_table()), jnp.asarray(wide_table()), sent.reshape(-1, LANES))


def shared_kernel(tall_ref, wide_ref, values_ref, numbers_ref, momentum_ref, left_ref):
    groups = values_ref.shape[0]
    lane_tile = lax.broadcasted_iota(jnp.int32, (1, LANES), 1) // KEPT
    for group in range(groups):
        columns = slice(group * WIDE, (group + 1) * WIDE)
        row, column, high, low = parts_of(numbers_ref[group : group + 1, :], values_ref[group : group + 1, :])
        weighted, hot = one_hots(row, column, high, low)
        hot = jnp.concatenate([jnp.where(lane_tile == tile, hot, jnp.zeros((), BF16)) for tile in range(GROUP)], 0)
        dense = lax.dot_general(weighted, hot, NT, preferred_element_type=F32)
        dense = dense[:TILE] + dense[TILE:]
        left_ref[:, columns] = BETA_DECAY * momentum_ref[:, columns] - back(dense, tall_ref[...], wide_ref[...])


def shared(values, numbers, momentum):
    return pl.pallas_call(
        shared_kernel,
        out_shape=jax.ShapeDtypeStruct(momentum.shape, F32),
        compiler_params=pltpu.CompilerParams(vmem_limit_bytes=32 * 2**20),
        cost_estimate=pl.CostEstimate(flops=4 * 10**8, bytes_accessed=2**20, transcendentals=0),
        name="shared",
    )(jnp.asarray(tall_table()), jnp.asarray(wide_table()), values, numbers, momentum)


FSDP = ("x", "core")


def copies_to(block, axis):
    count = lax.axis_size(axis)
    return lax.all_to_all(jnp.broadcast_to(block[None], (count,) + block.shape), axis, 0, 0, tiled=True)


def core_blocks(grads, core, columns):
    blocks = [grads[:, first : first + columns] for first in range(0, grads.shape[1], columns)]
    pairs = zip(blocks[::2], blocks[1::2], strict=True)
    return jnp.stack([jnp.where(core == 0, even, odd).astype(F32) for even, odd in pairs])


def others_of(blocks):
    count = blocks.shape[0]
    chip = lax.axis_index("x")
    taken = []
    for step in (2, 1, 3, 0):
        block = lax.dynamic_index_in_dim(blocks, (chip + step) % count, 0, keepdims=False)
        if step:
            block = lax.ppermute(block, "x", [(i, (i + step) % count) for i in range(count)])
        taken.append(block)
    return taken


def on_device(partial_grads, momentum_old, indices):
    groups = indices.shape[2] // GROUP
    grads, momentum = partial_grads[0, 0], momentum_old[0]
    columns = momentum.shape[1]
    core = lax.axis_index("core")
    own_numbers = indices.reshape(groups, LANES)
    numbers = copies_to(own_numbers, FSDP)
    other = core_blocks(grads, 1 - core, columns)
    own_part = pick_own(momentum, own_numbers)
    numbers, other, own_part = lax.optimization_barrier((numbers, other, own_part))
    arrived = lax.ppermute(other, "core", [(0, 1), (1, 0)])
    values = pick(grads, numbers)
    values = lax.all_to_all(values, FSDP, 0, 0, tiled=True)
    chip_sums = core_blocks(grads, core, columns) + arrived
    values, chip_sums = lax.optimization_barrier((values, chip_sums))
    parts = others_of(chip_sums)
    selected = jnp.sum(values, axis=0) + own_part
    own = jnp.concatenate(
        [jnp.pad(part, ((0, SLAB // 2 - groups), (0, 0))) for part in (selected, own_numbers.astype(F32))], 0
    )
    sent = copies_to(own, "z")
    left = shared(selected, own_numbers, momentum)
    sent, left = lax.optimization_barrier((sent, left))
    sent = copies_to(sent, "y")
    update = spread(sent, columns)
    fresh = left + sum(parts)
    return fresh[None], update


def solution(mesh):
    fine = jax.sharding.Mesh(mesh.devices.reshape(4, 16, 4, 2), ("y", "z", "x", "core"))
    rep = ("y", "z")
    in_specs = (P(rep, FSDP, None, None), P(rep, None, FSDP), P(rep, None, FSDP, None))
    out_specs = (P(rep, None, FSDP), P(None, FSDP))
    return jax.shard_map(on_device, mesh=fine, in_specs=in_specs, out_specs=out_specs, check_vma=False)
```

time: 108 us -> 85 us (0.79)
  the two profiles are of different devices: /device:TPU:32 before, /device:TPU:1 now
where the time goes in v3:
time: 85 us; the launch traced here: 84.2 us
  starting transfers between devices  41 us (48%)
  Pallas kernels  18 us (21%)
  waiting for transfers between devices  12.8 us (15%)
  other arithmetic  7.46 us (9%)
  local copies, waits for them, and re-layouts  4.15 us (5%)
  between operations  0.86 us (1%)
    all_to_all x3, starting transfers between devices, copies_to(): lax.all_to_all(jnp.broadcast_to(block[None], (count,) + block.shape), axi...  24.9 us
    ppermute x3, waiting for transfers between devices, others_of(): lax.ppermute(block, 'x', [(i, (i + step) % count) for i in range(count)])  9.96 us
    ppermute x3, starting transfers between devices, others_of(): lax.ppermute(block, 'x', [(i, (i + step) % count) for i in range(count)])  9.2 us
    pallas_call x1, Pallas kernels, spread(): pl.pallas_call(spread_kernel, out_shape=jax.ShapeDtypeStruct((TILE, colum...  7.43 us
    pallas_call x1, Pallas kernels, pick(): pl.pallas_call(pick_kernel, grid=(parts,), in_specs=[pl.BlockSpec((4 * TI...  7.32 us
    all_to_all x1, starting transfers between devices, on_device(): values = lax.all_to_all(values, FSDP, 0, 0, tiled=True)  4.59 us
    all_to_all x1, waiting for transfers between devices, on_device(): values = lax.all_to_all(values, FSDP, 0, 0, tiled=True)  2.79 us
    another operation x2, other arithmetic, core_blocks(): jnp.stack([jnp.where(core == 0, even, odd).astype(F32) for even, odd in p...  2.61 us
  transfers between devices with their start and end apart: 8, of which 2 were waited for; matrix products, arithmetic and copies ran while one was open for 10% of the time, Pallas kernels for 13%

profile of v3, /device:TPU:1, one launch (start us, length us, event | category | flops | bytes accessed | tf_op | source)
XLA Modules:
  0.0 84.2 jit_solution(17813776026533306285)
XLA Ops:
  0.6 0.8 reduce
  1.5 0.6 broadcast_in_dim.11
  2.1 10.1 %all-to-all-start = ((s32[8,7,128]{2,1,0:T(8,128)}), s32[8,7,128]{2,1,0:T(8,128)S(1)}, u32[]{:S(2)}, u32[]{:S(2)}) async-start(s32[8,7,128]{2,1,0:T(8,128)} %broadcast_in_dim.11), calls=%async_computation | async-start | bytes 65536 | tf_op jit(solution)/shard_map/all_to_all | solution.py:232
  12.2 2.5 %select_bitcast_fusion.3 = (bf16[1,64,1792]{2,1,0:T(8,128)(2,1)S(1)}, bf16[1,64,1792]{2,1,0:T(8,128)(2,1)S(1)}, bf16[1,64,1792]{2,1,0:T(8,128)(2,1)S(1)}, bf16[1...) fusion(pred[]{:T(512)S(6)} %eq.18, ...), kind=kLoop, calls=%fused_computation.11 | loop fusion | flops 917504 | bytes 3670018 | tf_op jit(solution)/shard_map/stack | solution.py:238
  14.6 0.2 maximum_convert_fusion
  14.8 0.8 %copy-done = f32[1,64,1792]{2,1,0:T(8,128)S(1)} copy-done((f32[1,64,1792]{2,1,0:T(8,128)S(1)}, f32[1,64,1792]{2,1,0:T(8,128)}, u32[]{:S(2)}) %copy-start) | copy-done | bytes 458776
  15.7 1.6 %pick_own.1 = f32[7,128]{1,0:T(8,128)S(1)} custom-call(bf16[256,128]{1,0:T(8,128)(2,1)S(1)} %copy-done.2, f32[64,1792]{1,0:T(8,128)S(1)} %bitcast.34, s32[7,128]{1,0:T(8,128)S(1)} %broadcast_in_dim.10.numbers_ref), custom_call_target="tpu_custom_call" | custom-call | flops 400000000 | bytes 524288 | tf_op jit(solution)/shard_map/pick_own/pallas_call | solution.py:96
  17.2 2.3 %collective-permute-start = (f32[4,64,1792]{2,1,0:T(8,128)S(1)}, f32[4,64,1792]{2,1,0:T(8,128)}, u32[]{:S(2)}, u32[]{:S(2)}) collective-permute-start(f32[4,64,1792]{2,1,0:T(8,128)S(1)} %maximum_convert_fusion), channel_id=1, source_target_pairs={{0,1},{1,0},{2,3},{3,2},{4,5},{5,4},{6,7},{7,6},{8,9},{9,8},{10,11... | collective-permute-start | bytes 5505032 | tf_op jit(solution)/shard_map/ppermute | solution.py:263
  19.6 7.3 %pick.1 = f32[8,7,128]{2,1,0:T(8,128)} custom-call(bf16[256,128]{1,0:T(8,128)(2,1)} %constant.58.clone.table_ref, bf16[64,14336]{1,0:T(8,128)(2,1)} %bitcast.37, s32[8,7,128]{2,1,0:T(8,128)} %copy-done.4), custom_call_target="tpu_custom_call" | custom-call | flops 2000000000 | bytes 2097152 | tf_op jit(solution)/shard_map/pick/pallas_call | solution.py:108
  27.0 4.6 %all-to-all-start.1 = ((f32[8,7,128]{2,1,0:T(8,128)}), f32[8,7,128]{2,1,0:T(8,128)S(1)}, u32[]{:S(2)}, u32[]{:S(2)}) async-start(f32[8,7,128]{2,1,0:T(8,128)} %pick.1), calls=%async_computation.1 | async-start | bytes 65536 | tf_op jit(solution)/shard_map/all_to_all | solution.py:265
  31.6 1.9 %convert_add_fusion = f32[4,64,1792]{2,1,0:T(8,128)S(1)} fusion(f32[4,64,1792]{2,1,0:T(8,128)} %collective-permute-done, bf16[1,64,1792]{2,1,0:T(8,128)(2,1)} %get-tuple-element.26, bf16[1,64,1792]{2,1,0:T(8,128)(2,1)} %get-tuple-element.25, bf16[1,64,1792]{2,1,0:T(8,128)(2,1)} %get-tuple-element.24, bf16[1,64,1792]{2,1,0:T(8,128)(2,1)S(1)} %get-tuple-element.19), kind=kLoop, calls=%fused_computation | loop fusion | flops 2293760 | bytes 4587520 | tf_op jit(solution)/shard_map/add | solution.py:266
  33.5 2.8 %all-to-all-done.1 = f32[8,7,128]{2,1,0:T(8,128)S(1)} async-done(((f32[8,7,128]{2,1,0:T(8,128)}), f32[8,7,128]{2,1,0:T(8,128)S(1)}, u32[]{:S(2)}, u32[]{:S(2)}) %all-to-all-start.1) | async-done | bytes 28704 | tf_op jit(solution)/shard_map/all_to_all | solution.py:265
  36.3 0.7 broadcast_in_dim.24
  37.0 10.6 %all-to-all-start.2 = ((f32[16,16,128]{2,1,0:T(8,128)}), f32[16,16,128]{2,1,0:T(8,128)S(1)}, u32[]{:S(2)}, u32[]{:S(2)}) async-start(f32[16,16,128]{2,1,0:T(8,128)} %broadcast_in_dim.24), calls=%async_computation.2 | async-start | bytes 262144 | tf_op jit(solution)/shard_map/all_to_all | solution.py:232
  47.6 1.1 %dynamic-slice_bitcast_fusion.1 = (f32[64,1792]{1,0:T(8,128)}, f32[64,1792]{1,0:T(8,128)}, f32[64,1792]{1,0:T(8,128)}) fusion(f32[4,64,1792]{2,1,0:T(8,128)S(1)} %convert_add_fusion, s32[]{:T(128)S(6)} %select_n.83, s32[]{:T(128)S(6)} %select_n.85, s32[]{:T(128)S(6)} %select_n.81), kind=kLoop, calls=%fused_computation.6 | loop fusion | bytes 2752524 | tf_op jit(solution)/shard_map/jit(dynamic_index_in_dim)/squeeze | solution.py:246
  48.7 2.7 %collective-permute-start.1 = (f32[64,1792]{1,0:T(8,128)}, f32[64,1792]{1,0:T(8,128)}, u32[]{:S(2)}, u32[]{:S(2)}) collective-permute-start(f32[64,1792]{1,0:T(8,128)} %get-tuple-element.18), channel_id=1, source_target_pairs={{0,4},{2,6},{4,0},{6,2},{1,5},{3,7},{5,1},{7,3},{8,12},{10,14},{12... | collective-permute-start | bytes 1376264 | tf_op jit(solution)/shard_map/ppermute | solution.py:248
  51.4 2.6 %collective-permute-start.2 = (f32[64,1792]{1,0:T(8,128)}, f32[64,1792]{1,0:T(8,128)}, u32[]{:S(2)}, u32[]{:S(2)}) collective-permute-start(f32[64,1792]{1,0:T(8,128)} %get-tuple-element.16), channel_id=1, source_target_pairs={{0,2},{2,4},{4,6},{6,0},{1,3},{3,5},{5,7},{7,1},{8,10},{10,12},{12... | collective-permute-start | bytes 1376264 | tf_op jit(solution)/shard_map/ppermute | solution.py:248
  53.9 3.9 %collective-permute-start.3 = (f32[64,1792]{1,0:T(8,128)}, f32[64,1792]{1,0:T(8,128)}, u32[]{:S(2)}, u32[]{:S(2)}) collective-permute-start(f32[64,1792]{1,0:T(8,128)} %get-tuple-element.17), channel_id=1, source_target_pairs={{0,6},{2,0},{4,2},{6,4},{1,7},{3,1},{5,3},{7,5},{8,14},{10,8},{12,... | collective-permute-start | bytes 1376264 | tf_op jit(solution)/shard_map/ppermute | solution.py:248
  57.9 1.7 %shared.1 = f32[64,1792]{1,0:T(8,128)S(1)} custom-call(bf16[64,192]{1,0:T(8,128)(2,1)S(1)} %copy-done.3, bf16[512,256]{1,0:T(8,128)(2,1)S(1)} %copy-done.1, f32[7,128]{1,0:T(8,128)S(1)} %add.58.values_ref, s32[7,128]{1,0:T(8,128)S(1)} %broadcast_in_dim.10.numbers_ref, f32[64,1792]{1,0:T(8,128)S(1)} %bitcast.35), custom_call_target="tpu_custom_call" | custom-call | flops 400000000 | bytes 1048576 | tf_op jit(solution)/shard_map/shared/pallas_call | solution.py:218
  59.7 0.8 broadcast_in_dim.26
  60.5 4.2 %all-to-all-start.3 = ((f32[4,16,16,128]{3,2,1,0:T(8,128)}), f32[4,16,16,128]{3,2,1,0:T(8,128)S(1)}, u32[]{:S(2)}, u32[]{:S(2)}) async-start(f32[4,16,16,128]{3,2,1,0:T(8,128)} %broadcast_in_dim.26), calls=%async_computation.3 | async-start | bytes 1048576 | tf_op jit(solution)/shard_map/all_to_all | solution.py:232
  64.7 10.0 %collective-permute-done.2 = f32[64,1792]{1,0:T(8,128)} collective-permute-done((f32[64,1792]{1,0:T(8,128)}, f32[64,1792]{1,0:T(8,128)}, u32[]{:S(2)}, u32[]{:S(2)}) %collective-permute-start.2) | collective-permute-done | bytes 458784 | tf_op jit(solution)/shard_map/ppermute | solution.py:248
  74.6 2.2 %fusion.1 = f32[1,64,1792]{2,1,0:T(8,128)} fusion(f32[64,1792]{1,0:T(8,128)S(1)} %shared.1, f32[4,64,1792]{2,1,0:T(8,128)S(1)} %convert_add_fusion, s32[]{:T(128)S(6)} %select_n.87, f32[64,1792]{1,0:T(8,128)} %collective-permute-done.3, f32[64,1792]{1,0:T(8,128)} %collective-permute-done.1, f32[64,1792]{1,0:T(8,128)} %collective-permute-done.2), kind=kLoop, calls=%fused_computation.4 | loop fusion | flops 458752 | bytes 2752516 | tf_op jit(solution)/shard_map/broadcast_in_dim | solution.py:279
  76.8 7.4 %spread.1 = f32[64,1792]{1,0:T(8,128)} custom-call(bf16[64,192]{1,0:T(8,128)(2,1)S(1)} %copy-done.3, bf16[512,256]{1,0:T(8,128)(2,1)S(1)} %copy-done.1, f32[1024,128]{1,0:T(8,128)S(1)} %bitcast.33), custom_call_target="tpu_custom_call" | custom-call | flops 2000000000 | bytes 1048576 | tf_op jit(solution)/shard_map/spread/pallas_call | solution.py:194
  (20 shorter events, 0.1 us)
Async XLA Ops:
  2.1 15.2 %all-to-all-start = ((s32[8,7,128]{2,1,0:T(8,128)}), s32[8,7,128]{2,1,0:T(8,128)S(1)}, u32[]{:S(2)}, u32[]{:S(2)}) async-start(s32[8,7,128]{2,1,0:T(8,128)} %broadcast_in_dim.11), calls=%async_computation | async-start | bytes 65536 | tf_op jit(solution)/shard_map/all_to_all | solution.py:232
  14.6 1.0 %copy-start = (f32[1,64,1792]{2,1,0:T(8,128)S(1)}, f32[1,64,1792]{2,1,0:T(8,128)}, u32[]{:S(2)}) copy-start(f32[1,64,1792]{2,1,0:T(8,128)} %param.10) | copy-start | bytes 1376260
  14.6 1.0 %copy-start.2 = (bf16[256,128]{1,0:T(8,128)(2,1)S(1)}, bf16[256,128]{1,0:T(8,128)(2,1)}, u32[]{:S(2)}) copy-start(bf16[256,128]{1,0:T(8,128)(2,1)} %constant.58.clone.table_ref) | copy-start | bytes 196612
  17.2 2.4 %copy-start.4 = (s32[8,7,128]{2,1,0:T(8,128)}, s32[8,7,128]{2,1,0:T(8,128)S(1)}, u32[]{:S(2)}) copy-start(s32[8,7,128]{2,1,0:T(8,128)S(1)} %all-to-all-done.numbers_ref) | copy-start | bytes 86020
  17.2 14.3 %collective-permute-start = (f32[4,64,1792]{2,1,0:T(8,128)S(1)}, f32[4,64,1792]{2,1,0:T(8,128)}, u32[]{:S(2)}, u32[]{:S(2)}) collective-permute-start(f32[4,64,1792]{2,1,0:T(8,128)S(1)} %maximum_convert_fusion), channel_id=1, source_target_pairs={{0,1},{1,0},{2,3},{3,2},{4,5},{5,4},{6,7},{7,6},{8,9},{9,8},{10,11... | collective-permute-start | bytes 5505032 | tf_op jit(solution)/shard_map/ppermute | solution.py:263
  27.0 9.3 %all-to-all-start.1 = ((f32[8,7,128]{2,1,0:T(8,128)}), f32[8,7,128]{2,1,0:T(8,128)S(1)}, u32[]{:S(2)}, u32[]{:S(2)}) async-start(f32[8,7,128]{2,1,0:T(8,128)} %pick.1), calls=%async_computation.1 | async-start | bytes 65536 | tf_op jit(solution)/shard_map/all_to_all | solution.py:265
  33.4 24.4 %copy-start.1 = (bf16[512,256]{1,0:T(8,128)(2,1)S(1)}, bf16[512,256]{1,0:T(8,128)(2,1)}, u32[]{:S(2)}) copy-start(bf16[512,256]{1,0:T(8,128)(2,1)} %constant.60.clone.wide_ref) | copy-start | bytes 786436
  33.5 24.4 %copy-start.3 = (bf16[64,192]{1,0:T(8,128)(2,1)S(1)}, bf16[64,192]{1,0:T(8,128)(2,1)}, u32[]{:S(2)}) copy-start(bf16[64,192]{1,0:T(8,128)(2,1)} %constant.59.clone.tall_ref) | copy-start | bytes 73732
  37.0 22.7 %all-to-all-start.2 = ((f32[16,16,128]{2,1,0:T(8,128)}), f32[16,16,128]{2,1,0:T(8,128)S(1)}, u32[]{:S(2)}, u32[]{:S(2)}) async-start(f32[16,16,128]{2,1,0:T(8,128)} %broadcast_in_dim.24), calls=%async_computation.2 | async-start | bytes 262144 | tf_op jit(solution)/shard_map/all_to_all | solution.py:232
  48.7 16.0 %collective-permute-start.1 = (f32[64,1792]{1,0:T(8,128)}, f32[64,1792]{1,0:T(8,128)}, u32[]{:S(2)}, u32[]{:S(2)}) collective-permute-start(f32[64,1792]{1,0:T(8,128)} %get-tuple-element.18), channel_id=1, source_target_pairs={{0,4},{2,6},{4,0},{6,2},{1,5},{3,7},{5,1},{7,3},{8,12},{10,14},{12... | collective-permute-start | bytes 1376264 | tf_op jit(solution)/shard_map/ppermute | solution.py:248
  51.4 23.3 %collective-permute-start.2 = (f32[64,1792]{1,0:T(8,128)}, f32[64,1792]{1,0:T(8,128)}, u32[]{:S(2)}, u32[]{:S(2)}) collective-permute-start(f32[64,1792]{1,0:T(8,128)} %get-tuple-element.16), channel_id=1, source_target_pairs={{0,2},{2,4},{4,6},{6,0},{1,3},{3,5},{5,7},{7,1},{8,10},{10,12},{12... | collective-permute-start | bytes 1376264 | tf_op jit(solution)/shard_map/ppermute | solution.py:248
  53.9 20.7 %collective-permute-start.3 = (f32[64,1792]{1,0:T(8,128)}, f32[64,1792]{1,0:T(8,128)}, u32[]{:S(2)}, u32[]{:S(2)}) collective-permute-start(f32[64,1792]{1,0:T(8,128)} %get-tuple-element.17), channel_id=1, source_target_pairs={{0,6},{2,0},{4,2},{6,4},{1,7},{3,1},{5,3},{7,5},{8,14},{10,8},{12,... | collective-permute-start | bytes 1376264 | tf_op jit(solution)/shard_map/ppermute | solution.py:248
  60.5 16.3 %all-to-all-start.3 = ((f32[4,16,16,128]{3,2,1,0:T(8,128)}), f32[4,16,16,128]{3,2,1,0:T(8,128)S(1)}, u32[]{:S(2)}, u32[]{:S(2)}) async-start(f32[4,16,16,128]{3,2,1,0:T(8,128)} %broadcast_in_dim.26), calls=%async_computation.3 | async-start | bytes 1048576 | tf_op jit(solution)/shard_map/all_to_all | solution.py:232

commit v4 on v3

--- a/solution.py
+++ b/solution.py
@@ -15,7 +15,7 @@
 GROUP = LANES // KEPT
 WIDE = GROUP * TILE
 BETA_DECAY = 0.999
-WHOLE_VMEM = 60 * 2**20
+FAR_RUNS = 4
 F32 = jnp.float32
 BF16 = jnp.bfloat16
 
@@ -77,11 +77,12 @@
 
 
 def pick_kernel(table_ref, grads_ref, numbers_ref, values_ref):
-    groups = numbers_ref.shape[1]
-    for group in range(groups):
-        columns = slice(group * WIDE, (group + 1) * WIDE)
-        down, across = cosine_rows(table_ref[...], numbers_ref[0, group : group + 1, :])
-        values_ref[0, group : group + 1, :] = picked(grads_ref[:, columns], down, across)
+    parts, groups, _ = numbers_ref.shape
+    for part in range(parts):
+        for group in range(groups):
+            first = (part * groups + group) * WIDE
+            down, across = cosine_rows(table_ref[...], numbers_ref[part, group : group + 1, :])
+            values_ref[part, group : group + 1, :] = picked(grads_ref[:, first : first + WIDE], down, across)
 
 
 def own_kernel(table_ref, momentum_ref, numbers_ref, own_ref):
@@ -103,22 +104,55 @@
 
 
 def pick(grads, numbers):
-    parts, groups, _ = numbers.shape
-    rows, columns = grads.shape
     return pl.pallas_call(
         pick_kernel,
-        grid=(parts,),
-        in_specs=[
-            pl.BlockSpec((4 * TILE, LANES), lambda i: (0, 0)),
-            pl.BlockSpec((rows, columns // parts), lambda i: (0, i)),
-            pl.BlockSpec((1, groups, LANES), lambda i: (i, 0, 0)),
-        ],
-        out_specs=pl.BlockSpec((1, groups, LANES), lambda i: (i, 0, 0)),
-        out_shape=jax.ShapeDtypeStruct((parts, groups, LANES), F32),
+        out_shape=jax.ShapeDtypeStruct(numbers.shape, F32),
         cost_estimate=pl.CostEstimate(flops=2 * 10**9, bytes_accessed=2**21, transcendentals=0),
-        compiler_params=pltpu.CompilerParams(vmem_limit_bytes=WHOLE_VMEM),
+        compiler_params=pltpu.CompilerParams(vmem_limit_bytes=16 * 2**20),
         name="pick",
     )(jnp.asarray(pick_table()), grads, numbers)
+
+
+def block_of(grads_ref, chip, core, step, parts, columns):
+    first = (2 * lax.rem(chip + step, parts) + core) * columns
+    return grads_ref[:, pl.ds(pl.multiple_of(first, LANES), columns)].astype(F32)
+
+
+def widen_kernel(at_ref, grads_ref, other_ref):
+    parts, _, columns = other_ref.shape
+    for step in range(parts):
+        other_ref[step] = block_of(grads_ref, at_ref[0], 1 - at_ref[1], step, parts, columns)
+
+
+def widen(at, grads, parts):
+    rows, columns = grads.shape
+    return pl.pallas_call(
+        widen_kernel,
+        in_specs=[pl.BlockSpec(memory_space=pltpu.SMEM), pl.BlockSpec(memory_space=pltpu.VMEM)],
+        out_shape=jax.ShapeDtypeStruct((parts, rows, columns // (2 * parts)), F32),
+        cost_estimate=pl.CostEstimate(flops=10**6, bytes_accessed=3 * 2**20, transcendentals=0),
+        compiler_params=pltpu.CompilerParams(vmem_limit_bytes=16 * 2**20),
+        name="widen",
+    )(at, grads)
+
+
+def add_kernel(at_ref, grads_ref, arrived_ref, *total_refs):
+    parts, _, columns = arrived_ref.shape
+    for step, total_ref in enumerate(total_refs):
+        total_ref[...] = block_of(grads_ref, at_ref[0], at_ref[1], step, parts, columns) + arrived_ref[step]
+
+
+def add_own(at, grads, arrived):
+    parts, rows, columns = arrived.shape
+    vmem = pl.BlockSpec(memory_space=pltpu.VMEM)
+    return pl.pallas_call(
+        add_kernel,
+        in_specs=[pl.BlockSpec(memory_space=pltpu.SMEM), vmem, vmem],
+        out_shape=[jax.ShapeDtypeStruct((rows, columns), F32)] * parts,
+        cost_estimate=pl.CostEstimate(flops=10**6, bytes_accessed=5 * 2**20, transcendentals=0),
+        compiler_params=pltpu.CompilerParams(vmem_limit_bytes=16 * 2**20),
+        name="add_own",
+    )(at, grads, arrived)
 
 
 def parts_of(numbers, values):
@@ -143,20 +177,24 @@
 NT = (((1,), (1,)), ((), ()))
 
 
-def back(dense, tall, wide):
-    high, low = halves(dense)
-    half = jnp.dot(tall, jnp.concatenate([high, high, low], 0), preferred_element_type=F32)
+def back(tiles, tall, wide):
+    count = len(tiles)
+    high, low = halves(jnp.concatenate(tiles, 0))
+    both = jnp.dot(jnp.concatenate([high, low], 0), wide[:WIDE], preferred_element_type=F32)
+    half = both[: TILE * count] + both[TILE * count :] + jnp.dot(high, wide[WIDE:], preferred_element_type=F32)
     high, low = halves(half)
-    both = jnp.dot(jnp.concatenate([high, low], 0), wide[:WIDE], preferred_element_type=F32)
-    return both[:TILE] + both[TILE:] + jnp.dot(high, wide[WIDE:], preferred_element_type=F32)
+    out = []
+    for first in range(0, TILE * count, TILE):
+        part = slice(first, first + TILE)
+        out.append(jnp.dot(tall, jnp.concatenate([high[part], high[part], low[part]], 0), preferred_element_type=F32))
+    return out
 
 
 def by_tile(block):
-    lane_part = lax.broadcasted_iota(jnp.int32, (SLAB, LANES), 1) // KEPT
-    rows = [block[SLAB * part : SLAB * (part + 1)] for part in range(GROUP)]
+    lane_part = lax.broadcasted_iota(jnp.int32, block[0].shape, 1) // KEPT
     tiles = []
     for tile in range(GROUP):
-        moved = [pltpu.roll(rows[p], (KEPT * (p - tile)) % LANES, 1) if p != tile else rows[p] for p in range(GROUP)]
+        moved = [pltpu.roll(block[p], (KEPT * (p - tile)) % LANES, 1) if p != tile else block[p] for p in range(GROUP)]
         total = moved[0]
         for part in range(1, GROUP):
             total = jnp.where(lane_part == part, moved[part], total)
@@ -175,43 +213,75 @@
     return total[:TILE] + total[TILE:]
 
 
-def spread_kernel(tall_ref, wide_ref, sent_ref, update_ref, rows_ref):
-    groups = update_ref.shape[1] // WIDE
-    replicas = sent_ref.shape[0] // SLAB
-    for group in range(groups):
-        values = by_tile(sent_ref[pl.ds(group, replicas, stride=SLAB), :])
-        numbers = by_tile(sent_ref[pl.ds(SLAB // 2 + group, replicas, stride=SLAB), :])
+def dense_group(sent_ref, rows_ref, group, firsts, replicas):
+    count = replicas // GROUP
+    for run, first in enumerate(firsts):
+
+        def rows(offset):
+            starts = [first + part * SLAB + offset for part in range(GROUP)]
+            return by_tile([sent_ref[pl.ds(start, count, stride=GROUP * SLAB), :] for start in starts])
+
+        values, numbers = rows(group), rows(SLAB // 2 + group)
         for tile in range(GROUP):
             for part, value in enumerate(parts_of(numbers[tile], values[tile])):
-                rows_ref[group % 2, tile, part] = value
-        dense = [scattered(rows_ref.at[group % 2, tile], SLAB) for tile in range(GROUP)]
-        update_ref[:, group * WIDE : (group + 1) * WIDE] = back(
-            jnp.concatenate(dense, 1), tall_ref[...], wide_ref[...]
-        )
-
-
-def spread(sent, columns):
-    return pl.pallas_call(
-        spread_kernel,
+                rows_ref[group % 2, tile, part, run * count : (run + 1) * count, :] = value
+    tiles = [scattered(rows_ref.at[group % 2, tile], count * len(firsts)) for tile in range(GROUP)]
+    return jnp.concatenate(tiles, 1)
+
+
+def near_kernel(sent_ref, dense_ref, rows_ref):
+    for group in range(dense_ref.shape[1] // WIDE):
+        columns = slice(group * WIDE, (group + 1) * WIDE)
+        dense_ref[:, columns] = dense_group(sent_ref, rows_ref, group, [0], sent_ref.shape[0] // SLAB)
+
+
+def near(sent, columns):
+    return pl.pallas_call(
+        near_kernel,
         out_shape=jax.ShapeDtypeStruct((TILE, columns), F32),
         scratch_shapes=[pltpu.VMEM((2, GROUP, 4, SLAB, LANES), F32)],
-        compiler_params=pltpu.CompilerParams(vmem_limit_bytes=32 * 2**20),
+        compiler_params=pltpu.CompilerParams(vmem_limit_bytes=16 * 2**20),
+        cost_estimate=pl.CostEstimate(flops=10**9, bytes_accessed=2**20, transcendentals=0),
+        name="near",
+    )(sent.reshape(-1, LANES))
+
+
+def spread_kernel(at_ref, tall_ref, wide_ref, sent_ref, near_ref, update_ref, rows_ref):
+    length = sent_ref.shape[0] // FAR_RUNS
+    firsts = [pl.multiple_of(lax.rem(at_ref[0] + step, FAR_RUNS) * length, SLAB) for step in range(1, FAR_RUNS)]
+    dense = []
+    for group in range(near_ref.shape[1] // WIDE):
+        columns = slice(group * WIDE, (group + 1) * WIDE)
+        dense.append(near_ref[:, columns] + dense_group(sent_ref, rows_ref, group, firsts, length // SLAB))
+    for group, piece in enumerate(back(dense, tall_ref[...], wide_ref[...])):
+        update_ref[:, group * WIDE : (group + 1) * WIDE] = piece
+
+
+def spread(at, sent, dense):
+    vmem = pl.BlockSpec(memory_space=pltpu.VMEM)
+    return pl.pallas_call(
+        spread_kernel,
+        in_specs=[pl.BlockSpec(memory_space=pltpu.SMEM)] + [vmem] * 4,
+        out_shape=jax.ShapeDtypeStruct(dense.shape, F32),
+        scratch_shapes=[pltpu.VMEM((2, GROUP, 4, SLAB, LANES), F32)],
+        compiler_params=pltpu.CompilerParams(vmem_limit_bytes=16 * 2**20),
         cost_estimate=pl.CostEstimate(flops=2 * 10**9, bytes_accessed=2**20, transcendentals=0),
         name="spread",
-    )(jnp.asarray(tall_table()), jnp.asarray(wide_table()), sent.reshape(-1, LANES))
+    )(at, jnp.asarray(tall_table()), jnp.asarray(wide_table()), sent.reshape(-1, LANES), dense)
 
 
 def shared_kernel(tall_ref, wide_ref, values_ref, numbers_ref, momentum_ref, left_ref):
-    groups = values_ref.shape[0]
     lane_tile = lax.broadcasted_iota(jnp.int32, (1, LANES), 1) // KEPT
-    for group in range(groups):
-        columns = slice(group * WIDE, (group + 1) * WIDE)
+    tiles = []
+    for group in range(values_ref.shape[0]):
         row, column, high, low = parts_of(numbers_ref[group : group + 1, :], values_ref[group : group + 1, :])
         weighted, hot = one_hots(row, column, high, low)
         hot = jnp.concatenate([jnp.where(lane_tile == tile, hot, jnp.zeros((), BF16)) for tile in range(GROUP)], 0)
         dense = lax.dot_general(weighted, hot, NT, preferred_element_type=F32)
-        dense = dense[:TILE] + dense[TILE:]
-        left_ref[:, columns] = BETA_DECAY * momentum_ref[:, columns] - back(dense, tall_ref[...], wide_ref[...])
+        tiles.append(dense[:TILE] + dense[TILE:])
+    for group, piece in enumerate(back(tiles, tall_ref[...], wide_ref[...])):
+        columns = slice(group * WIDE, (group + 1) * WIDE)
+        left_ref[:, columns] = BETA_DECAY * momentum_ref[:, columns] - piece
 
 
 def shared(values, numbers, momentum):
@@ -232,51 +302,36 @@
     return lax.all_to_all(jnp.broadcast_to(block[None], (count,) + block.shape), axis, 0, 0, tiled=True)
 
 
-def core_blocks(grads, core, columns):
-    blocks = [grads[:, first : first + columns] for first in range(0, grads.shape[1], columns)]
-    pairs = zip(blocks[::2], blocks[1::2], strict=True)
-    return jnp.stack([jnp.where(core == 0, even, odd).astype(F32) for even, odd in pairs])
-
-
-def others_of(blocks):
-    count = blocks.shape[0]
-    chip = lax.axis_index("x")
-    taken = []
-    for step in (2, 1, 3, 0):
-        block = lax.dynamic_index_in_dim(blocks, (chip + step) % count, 0, keepdims=False)
-        if step:
-            block = lax.ppermute(block, "x", [(i, (i + step) % count) for i in range(count)])
-        taken.append(block)
-    return taken
-
-
 def on_device(partial_grads, momentum_old, indices):
     groups = indices.shape[2] // GROUP
     grads, momentum = partial_grads[0, 0], momentum_old[0]
-    columns = momentum.shape[1]
-    core = lax.axis_index("core")
+    chips = lax.axis_size("x")
+    at = jnp.stack([lax.axis_index("x"), lax.axis_index("core")]).astype(jnp.int32)
     own_numbers = indices.reshape(groups, LANES)
     numbers = copies_to(own_numbers, FSDP)
-    other = core_blocks(grads, 1 - core, columns)
+    other = widen(at, grads, chips)
     own_part = pick_own(momentum, own_numbers)
     numbers, other, own_part = lax.optimization_barrier((numbers, other, own_part))
     arrived = lax.ppermute(other, "core", [(0, 1), (1, 0)])
     values = pick(grads, numbers)
     values = lax.all_to_all(values, FSDP, 0, 0, tiled=True)
-    chip_sums = core_blocks(grads, core, columns) + arrived
+    chip_sums = add_own(at, grads, arrived)
     values, chip_sums = lax.optimization_barrier((values, chip_sums))
-    parts = others_of(chip_sums)
     selected = jnp.sum(values, axis=0) + own_part
     own = jnp.concatenate(
         [jnp.pad(part, ((0, SLAB // 2 - groups), (0, 0))) for part in (selected, own_numbers.astype(F32))], 0
     )
     sent = copies_to(own, "z")
+    parts = [chip_sums[0]]
+    for step in (2, 1, 3):
+        parts.append(lax.ppermute(chip_sums[step], "x", [(i, (i + step) % chips) for i in range(chips)]))
     left = shared(selected, own_numbers, momentum)
     sent, left = lax.optimization_barrier((sent, left))
-    sent = copies_to(sent, "y")
-    update = spread(sent, columns)
-    fresh = left + sum(parts)
-    return fresh[None], update
+    far = copies_to(sent, "y")
+    dense = near(sent, momentum.shape[1])
+    far, dense = lax.optimization_barrier((far, dense))
+    update = spread(lax.axis_index("y").astype(jnp.int32)[None], far, dense)
+    return (left + sum(parts))[None], update
 
 
 def solution(mesh):

time: 85 us -> 76.4 us (0.90)
  other arithmetic: 7.46 us -> 2.89 us
  Pallas kernels: 18 us -> 13.7 us
  waiting for transfers between devices: 12.8 us -> 10.3 us
  local copies, waits for them, and re-layouts: 4.15 us -> 6.5 us
    pallas_call x2 -> x5, Pallas kernels: 14.7 us -> 11.2 us  [the longest x1 4.42 us: spread(): pl.pallas_call(spread_kernel, in_specs=[pl.BlockSpec(memory_space=pltpu.S...]
    unnamed x10 -> x18, local copies, waits for them, and re-layouts: 0.87 us -> 4.31 us
    another operation x2 -> x1, other arithmetic: 2.61 us -> 0.07 us  [on_device(): jnp.stack([lax.axis_index('x'), lax.axis_index('core')]).astype(jnp.int32)]
    ppermute x3, waiting for transfers between devices: 9.96 us -> 7.68 us  [on_device(): lax.ppermute(chip_sums[step], 'x', [(i, (i + step) % chips) for i in rang...]
    add x1 -> x0, other arithmetic: 1.89 us -> none  [on_device(): chip_sums = core_blocks(grads, core, columns) + arrived]
    all_to_all x1, waiting for transfers between devices: 2.79 us -> 1.41 us  [on_device(): values = lax.all_to_all(values, FSDP, 0, 0, tiled=True)]
    all_to_all x3, waiting for transfers between devices: 0.01 us -> 1.2 us  [copies_to(): lax.all_to_all(jnp.broadcast_to(block[None], (count,) + block.shape), axi...]
    squeeze x1 -> x0, local copies, waits for them, and re-layouts: 1.1 us -> none  [others_of(): lax.dynamic_index_in_dim(blocks, (chip + step) % count, 0, keepdims=False)]
  transfers between devices with their start and end apart: 8 -> 8, of which waited for: 2 -> 3; matrix products, arithmetic and copies ran while one was open for 10% -> 4% of each run, Pallas kernels for 13% -> 12%
where the time goes in v4:
time: 76.4 us; the launch traced here: 75.8 us
  starting transfers between devices  41.7 us (55%)
  Pallas kernels  13.7 us (18%)
  waiting for transfers between devices  10.3 us (13%)
  local copies, waits for them, and re-layouts  6.5 us (9%)
  other arithmetic  2.89 us (4%)
  between operations  0.8 us (1%)
    all_to_all x3, starting transfers between devices, copies_to(): lax.all_to_all(jnp.broadcast_to(block[None], (count,) + block.shape), axi...  24.9 us
    ppermute x3, starting transfers between devices, on_device(): lax.ppermute(chip_sums[step], 'x', [(i, (i + step) % chips) for i in rang...  9.88 us
    ppermute x3, waiting for transfers between devices, on_device(): lax.ppermute(chip_sums[step], 'x', [(i, (i + step) % chips) for i in rang...  7.68 us
    all_to_all x1, starting transfers between devices, on_device(): values = lax.all_to_all(values, FSDP, 0, 0, tiled=True)  4.66 us
    pallas_call x1, Pallas kernels, spread(): pl.pallas_call(spread_kernel, in_specs=[pl.BlockSpec(memory_space=pltpu.S...  4.42 us
    unnamed x18, local copies, waits for them, and re-layouts  4.31 us
    pallas_call x1, Pallas kernels, pick(): pl.pallas_call(pick_kernel, out_shape=jax.ShapeDtypeStruct(numbers.shape,...  3.13 us
    ppermute x1, starting transfers between devices, on_device(): arrived = lax.ppermute(other, 'core', [(0, 1), (1, 0)])  2.26 us
  transfers between devices with their start and end apart: 8, of which 3 were waited for; matrix products, arithmetic and copies ran while one was open for 4% of the time, Pallas kernels for 12%

profile of v4, /device:TPU:1, one launch (start us, length us, event | category | flops | bytes accessed | tf_op | source)
XLA Modules:
  0.0 75.8 jit_solution(3199532438584477795)
XLA Ops:
  0.6 0.8 reduce
  2.1 10.1 %all-to-all-start = ((s32[8,7,128]{2,1,0:T(8,128)}), s32[8,7,128]{2,1,0:T(8,128)S(1)}, u32[]{:S(2)}, u32[]{:S(2)}) async-start(s32[8,7,128]{2,1,0:T(8,128)} %broadcast_in_dim.26), calls=%async_computation | async-start | bytes 65536 | tf_op jit(solution)/shard_map/all_to_all | solution.py:302
  12.3 1.5 %copy-done = bf16[1,1,64,14336]{3,2,1,0:T(8,128)(2,1)S(1)} copy-done((bf16[1,1,64,14336]{3,2,1,0:T(8,128)(2,1)S(1)}, bf16[1,1,64,14336]{3,2,1,0:T(8,128)(2,1)}, u32[]{:S(2)}) %copy-start) | copy-done | bytes 1835032
  14.5 1.3 %copy-done.2 = f32[4,64,1792]{2,1,0:T(8,128)} copy-done((f32[4,64,1792]{2,1,0:T(8,128)}, f32[4,64,1792]{2,1,0:T(8,128)S(1)}, u32[]{:S(2)}) %copy-start.2) | copy-done | bytes 1835032
  15.7 1.6 %pick_own.1 = f32[7,128]{1,0:T(8,128)S(1)} custom-call(bf16[256,128]{1,0:T(8,128)(2,1)S(1)} %copy-done.7, f32[64,1792]{1,0:T(8,128)S(1)} %bitcast.14, s32[7,128]{1,0:T(8,128)S(1)} %broadcast_in_dim.12.numbers_ref), custom_call_target="tpu_custom_call" | custom-call | flops 400000000 | bytes 524288 | tf_op jit(solution)/shard_map/pick_own/pallas_call | solution.py:97
  17.3 2.3 %collective-permute-start = (f32[4,64,1792]{2,1,0:T(8,128)}, f32[4,64,1792]{2,1,0:T(8,128)}, u32[]{:S(2)}, u32[]{:S(2)}) collective-permute-start(f32[4,64,1792]{2,1,0:T(8,128)} %copy-done.2), channel_id=1, source_target_pairs={{0,1},{1,0},{2,3},{3,2},{4,5},{5,4},{6,7},{7,6},{8,9},{9,8},{10,11... | collective-permute-start | bytes 5505032 | tf_op jit(solution)/shard_map/ppermute | solution.py:315
  19.6 3.1 %pick.1 = f32[8,7,128]{2,1,0:T(8,128)} custom-call(bf16[256,128]{1,0:T(8,128)(2,1)S(1)} %copy-done.7, bf16[64,14336]{1,0:T(8,128)(2,1)S(1)} %bitcast.10, s32[8,7,128]{2,1,0:T(8,128)S(1)} %all-to-all-done.numbers_ref), custom_call_target="tpu_custom_call" | custom-call | flops 2000000000 | bytes 2097152 | tf_op jit(solution)/shard_map/pick/pallas_call | solution.py:107
  22.7 4.7 %all-to-all-start.1 = ((f32[8,7,128]{2,1,0:T(8,128)}), f32[8,7,128]{2,1,0:T(8,128)S(1)}, u32[]{:S(2)}, u32[]{:S(2)}) async-start(f32[8,7,128]{2,1,0:T(8,128)} %pick.1), calls=%async_computation.1 | async-start | bytes 65536 | tf_op jit(solution)/shard_map/all_to_all | solution.py:317
  27.4 1.7 %add_own.1 = (f32[64,1792]{1,0:T(8,128)S(1)}, f32[64,1792]{1,0:T(8,128)S(1)}, f32[64,1792]{1,0:T(8,128)S(1)}, f32[64,1792]{1,0:T(8,128)S(1)}) custom-call(s32[2]{0:T(128)S(1)} %pad_add_fusion.at_ref, bf16[64,14336]{1,0:T(8,128)(2,1)S(1)} %bitcast.11, f32[4,64,1792]{2,1,0:T(8,128)} %collective-permute-done.arrived_ref), custom_call_target="tpu_custom_call" | custom-call | flops 1000000 | bytes 5242880 | tf_op jit(solution)/shard_map/add_own/pallas_call | solution.py:148
  29.2 0.8 copy-done.4
  29.9 0.8 %copy-done.5 = f32[64,1792]{1,0:T(8,128)} copy-done((f32[64,1792]{1,0:T(8,128)}, f32[64,1792]{1,0:T(8,128)S(1)}, u32[]{:S(2)}) %copy-start.5) | copy-done | bytes 458776
  30.7 1.4 %all-to-all-done.1 = f32[8,7,128]{2,1,0:T(8,128)S(1)} async-done(((f32[8,7,128]{2,1,0:T(8,128)}), f32[8,7,128]{2,1,0:T(8,128)S(1)}, u32[]{:S(2)}, u32[]{:S(2)}) %all-to-all-start.1) | async-done | bytes 28704 | tf_op jit(solution)/shard_map/all_to_all | solution.py:317
  32.8 10.6 %all-to-all-start.2 = ((f32[16,16,128]{2,1,0:T(8,128)}), f32[16,16,128]{2,1,0:T(8,128)S(1)}, u32[]{:S(2)}, u32[]{:S(2)}) async-start(f32[16,16,128]{2,1,0:T(8,128)} %broadcast_in_dim.27), calls=%async_computation.2 | async-start | bytes 262144 | tf_op jit(solution)/shard_map/all_to_all | solution.py:302
  43.4 3.4 %collective-permute-start.1 = (f32[64,1792]{1,0:T(8,128)}, f32[64,1792]{1,0:T(8,128)S(1)}, u32[]{:S(2)}, u32[]{:S(2)}) collective-permute-start(f32[64,1792]{1,0:T(8,128)} %copy-done.5), channel_id=1, source_target_pairs={{0,4},{2,6},{4,0},{6,2},{1,5},{3,7},{5,1},{7,3},{8,12},{10,14},{12... | collective-permute-start | bytes 1376264 | tf_op jit(solution)/shard_map/ppermute | solution.py:327
  46.8 2.2 %collective-permute-start.2 = (f32[64,1792]{1,0:T(8,128)}, f32[64,1792]{1,0:T(8,128)}, u32[]{:S(2)}, u32[]{:S(2)}) collective-permute-start(f32[64,1792]{1,0:T(8,128)} %copy-done.4), channel_id=1, source_target_pairs={{0,2},{2,4},{4,6},{6,0},{1,3},{3,5},{5,7},{7,1},{8,10},{10,12},{12... | collective-permute-start | bytes 1376264 | tf_op jit(solution)/shard_map/ppermute | solution.py:327
  49.0 4.3 %collective-permute-start.3 = (f32[64,1792]{1,0:T(8,128)S(1)}, f32[64,1792]{1,0:T(8,128)}, u32[]{:S(2)}, u32[]{:S(2)}) collective-permute-start(f32[64,1792]{1,0:T(8,128)S(1)} %get-tuple-element.30), channel_id=1, source_target_pairs={{0,6},{2,0},{4,2},{6,4},{1,7},{3,1},{5,3},{7,5},{8,14},{10,8},{12,... | collective-permute-start | bytes 1376264 | tf_op jit(solution)/shard_map/ppermute | solution.py:327
  53.3 0.9 %shared.1 = f32[64,1792]{1,0:T(8,128)S(1)} custom-call(bf16[64,192]{1,0:T(8,128)(2,1)S(1)} %copy-done.8, bf16[512,256]{1,0:T(8,128)(2,1)S(1)} %copy-done.6, f32[7,128]{1,0:T(8,128)S(1)} %add.19.values_ref, s32[7,128]{1,0:T(8,128)S(1)} %broadcast_in_dim.12.numbers_ref, f32[64,1792]{1,0:T(8,128)S(1)} %bitcast.15), custom_call_target="tpu_custom_call" | custom-call | flops 400000000 | bytes 1048576 | tf_op jit(solution)/shard_map/shared/pallas_call | solution.py:288
  54.2 1.2 %all-to-all-done.2 = f32[16,16,128]{2,1,0:T(8,128)S(1)} async-done(((f32[16,16,128]{2,1,0:T(8,128)}), f32[16,16,128]{2,1,0:T(8,128)S(1)}, u32[]{:S(2)}, u32[]{:S(2)}) %all-to-all-start.2) | async-done | bytes 131104 | tf_op jit(solution)/shard_map/all_to_all | solution.py:302
  55.4 0.8 %broadcast_in_dim.30 = f32[4,16,16,128]{3,2,1,0:T(8,128)} broadcast(f32[16,16,128]{2,1,0:T(8,128)S(1)} %all-to-all-done.2), dimensions={1,2,3} | broadcast | bytes 655360 | tf_op jit(solution)/shard_map/broadcast_in_dim | solution.py:302
  56.2 4.2 %all-to-all-start.3 = ((f32[4,16,16,128]{3,2,1,0:T(8,128)}), f32[4,16,16,128]{3,2,1,0:T(8,128)S(1)}, u32[]{:S(2)}, u32[]{:S(2)}) async-start(f32[4,16,16,128]{3,2,1,0:T(8,128)} %broadcast_in_dim.30), calls=%async_computation.3 | async-start | bytes 1048576 | tf_op jit(solution)/shard_map/all_to_all | solution.py:302
  60.4 1.3 %near.1.near_ref = f32[64,1792]{1,0:T(8,128)S(1)} custom-call(f32[256,128]{1,0:T(8,128)S(1)} %bitcast.12), custom_call_target="tpu_custom_call" | custom-call | flops 1000000000 | bytes 1048576 | tf_op jit(solution)/shard_map/near/pallas_call | solution.py:239
  61.7 7.7 %collective-permute-done.2 = f32[64,1792]{1,0:T(8,128)} collective-permute-done((f32[64,1792]{1,0:T(8,128)}, f32[64,1792]{1,0:T(8,128)}, u32[]{:S(2)}, u32[]{:S(2)}) %collective-permute-start.2) | collective-permute-done | bytes 458784 | tf_op jit(solution)/shard_map/ppermute | solution.py:327
  69.4 2.0 %add_bitcast_fusion = f32[1,64,1792]{2,1,0:T(8,128)} fusion(f32[64,1792]{1,0:T(8,128)S(1)} %shared.1, f32[64,1792]{1,0:T(8,128)} %collective-permute-done.3, f32[64,1792]{1,0:T(8,128)} %collective-permute-done.2, f32[64,1792]{1,0:T(8,128)S(1)} %get-tuple-element.27, f32[64,1792]{1,0:T(8,128)S(1)} %collective-permute-done.1), kind=kLoop, calls=%fused_computation | loop fusion | flops 458752 | bytes 2752512 | tf_op jit(solution)/shard_map/broadcast_in_dim | solution.py:334
  71.4 4.4 %spread.1 = f32[64,1792]{1,0:T(8,128)} custom-call(s32[1]{0:T(128)} %bitcast.5.at_ref, bf16[64,192]{1,0:T(8,128)(2,1)S(1)} %copy-done.8, bf16[512,256]{1,0:T(8,128)(2,1)S(1)} %copy-done.6, f32[1024,128]{1,0:T(8,128)S(1)} %bitcast.13, f32[64,1792]{1,0:T(8,128)S(1)} %near.1.near_ref), custom_call_target="tpu_custom_call" | custom-call | flops 2000000000 | bytes 1048576 | tf_op jit(solution)/shard_map/spread/pallas_call | solution.py:262
  (28 shorter events, 2.2 us)
Async XLA Ops:
  2.1 15.2 %all-to-all-start = ((s32[8,7,128]{2,1,0:T(8,128)}), s32[8,7,128]{2,1,0:T(8,128)S(1)}, u32[]{:S(2)}, u32[]{:S(2)}) async-start(s32[8,7,128]{2,1,0:T(8,128)} %broadcast_in_dim.26), calls=%async_computation | async-start | bytes 65536 | tf_op jit(solution)/shard_map/all_to_all | solution.py:302
  12.3 1.5 %copy-start = (bf16[1,1,64,14336]{3,2,1,0:T(8,128)(2,1)S(1)}, bf16[1,1,64,14336]{3,2,1,0:T(8,128)(2,1)}, u32[]{:S(2)}) copy-start(bf16[1,1,64,14336]{3,2,1,0:T(8,128)(2,1)} %param.9) | copy-start | bytes 5505028
  13.8 2.0 %copy-start.3 = (f32[1,64,1792]{2,1,0:T(8,128)S(1)}, f32[1,64,1792]{2,1,0:T(8,128)}, u32[]{:S(2)}) copy-start(f32[1,64,1792]{2,1,0:T(8,128)} %param.10) | copy-start | bytes 1376260
  13.8 2.0 %copy-start.7 = (bf16[256,128]{1,0:T(8,128)(2,1)S(1)}, bf16[256,128]{1,0:T(8,128)(2,1)}, u32[]{:S(2)}) copy-start(bf16[256,128]{1,0:T(8,128)(2,1)} %constant.22.clone.table_ref) | copy-start | bytes 196612
  13.8 5.8 %copy-start.1 = (bf16[1,1,64,14336]{3,2,1,0:T(8,128)(2,1)S(1)}, bf16[1,1,64,14336]{3,2,1,0:T(8,128)(2,1)}, u32[]{:S(2)}) copy-start(bf16[1,1,64,14336]{3,2,1,0:T(8,128)(2,1)} %param.9) | copy-start | bytes 5505028
  14.5 1.3 %copy-start.2 = (f32[4,64,1792]{2,1,0:T(8,128)}, f32[4,64,1792]{2,1,0:T(8,128)S(1)}, u32[]{:S(2)}) copy-start(f32[4,64,1792]{2,1,0:T(8,128)S(1)} %widen.1) | copy-start | bytes 5505028
  17.3 10.1 %collective-permute-start = (f32[4,64,1792]{2,1,0:T(8,128)}, f32[4,64,1792]{2,1,0:T(8,128)}, u32[]{:S(2)}, u32[]{:S(2)}) collective-permute-start(f32[4,64,1792]{2,1,0:T(8,128)} %copy-done.2), channel_id=1, source_target_pairs={{0,1},{1,0},{2,3},{3,2},{4,5},{5,4},{6,7},{7,6},{8,9},{9,8},{10,11... | collective-permute-start | bytes 5505032 | tf_op jit(solution)/shard_map/ppermute | solution.py:315
  22.7 9.4 %all-to-all-start.1 = ((f32[8,7,128]{2,1,0:T(8,128)}), f32[8,7,128]{2,1,0:T(8,128)S(1)}, u32[]{:S(2)}, u32[]{:S(2)}) async-start(f32[8,7,128]{2,1,0:T(8,128)} %pick.1), calls=%async_computation.1 | async-start | bytes 65536 | tf_op jit(solution)/shard_map/all_to_all | solution.py:317
  27.4 25.9 %copy-start.6 = (bf16[512,256]{1,0:T(8,128)(2,1)S(1)}, bf16[512,256]{1,0:T(8,128)(2,1)}, u32[]{:S(2)}) copy-start(bf16[512,256]{1,0:T(8,128)(2,1)} %constant.24.clone.wide_ref) | copy-start | bytes 786436
  27.4 25.9 %copy-start.8 = (bf16[64,192]{1,0:T(8,128)(2,1)S(1)}, bf16[64,192]{1,0:T(8,128)(2,1)}, u32[]{:S(2)}) copy-start(bf16[64,192]{1,0:T(8,128)(2,1)} %constant.23.clone.tall_ref) | copy-start | bytes 73732
  29.2 0.8 %copy-start.4 = (f32[64,1792]{1,0:T(8,128)}, f32[64,1792]{1,0:T(8,128)S(1)}, u32[]{:S(2)}) copy-start(f32[64,1792]{1,0:T(8,128)S(1)} %get-tuple-element.29) | copy-start | bytes 1376260
  29.9 0.8 %copy-start.5 = (f32[64,1792]{1,0:T(8,128)}, f32[64,1792]{1,0:T(8,128)S(1)}, u32[]{:S(2)}) copy-start(f32[64,1792]{1,0:T(8,128)S(1)} %get-tuple-element.28) | copy-start | bytes 1376260
  32.8 22.6 %all-to-all-start.2 = ((f32[16,16,128]{2,1,0:T(8,128)}), f32[16,16,128]{2,1,0:T(8,128)S(1)}, u32[]{:S(2)}, u32[]{:S(2)}) async-start(f32[16,16,128]{2,1,0:T(8,128)} %broadcast_in_dim.27), calls=%async_computation.2 | async-start | bytes 262144 | tf_op jit(solution)/shard_map/all_to_all | solution.py:302
  43.4 18.3 %collective-permute-start.1 = (f32[64,1792]{1,0:T(8,128)}, f32[64,1792]{1,0:T(8,128)S(1)}, u32[]{:S(2)}, u32[]{:S(2)}) collective-permute-start(f32[64,1792]{1,0:T(8,128)} %copy-done.5), channel_id=1, source_target_pairs={{0,4},{2,6},{4,0},{6,2},{1,5},{3,7},{5,1},{7,3},{8,12},{10,14},{12... | collective-permute-start | bytes 1376264 | tf_op jit(solution)/shard_map/ppermute | solution.py:327
  46.8 22.6 %collective-permute-start.2 = (f32[64,1792]{1,0:T(8,128)}, f32[64,1792]{1,0:T(8,128)}, u32[]{:S(2)}, u32[]{:S(2)}) collective-permute-start(f32[64,1792]{1,0:T(8,128)} %copy-done.4), channel_id=1, source_target_pairs={{0,2},{2,4},{4,6},{6,0},{1,3},{3,5},{5,7},{7,1},{8,10},{10,12},{12... | collective-permute-start | bytes 1376264 | tf_op jit(solution)/shard_map/ppermute | solution.py:327
  49.0 20.4 %collective-permute-start.3 = (f32[64,1792]{1,0:T(8,128)S(1)}, f32[64,1792]{1,0:T(8,128)}, u32[]{:S(2)}, u32[]{:S(2)}) collective-permute-start(f32[64,1792]{1,0:T(8,128)S(1)} %get-tuple-element.30), channel_id=1, source_target_pairs={{0,6},{2,0},{4,2},{6,4},{1,7},{3,1},{5,3},{7,5},{8,14},{10,8},{12,... | collective-permute-start | bytes 1376264 | tf_op jit(solution)/shard_map/ppermute | solution.py:327
  56.2 15.2 %all-to-all-start.3 = ((f32[4,16,16,128]{3,2,1,0:T(8,128)}), f32[4,16,16,128]{3,2,1,0:T(8,128)S(1)}, u32[]{:S(2)}, u32[]{:S(2)}) async-start(f32[4,16,16,128]{3,2,1,0:T(8,128)} %broadcast_in_dim.30), calls=%async_computation.3 | async-start | bytes 1048576 | tf_op jit(solution)/shard_map/all_to_all | solution.py:302

commit v5 on v4

--- a/solution.py
+++ b/solution.py
@@ -76,41 +76,27 @@
     return jnp.sum((mixed[:, :LANES] + mixed[:, LANES:]) * down, axis=0, keepdims=True)
 
 
-def pick_kernel(table_ref, grads_ref, numbers_ref, values_ref):
+def pick_kernel(table_ref, grads_ref, numbers_ref, momentum_ref, own_numbers_ref, values_ref, own_ref):
     parts, groups, _ = numbers_ref.shape
     for part in range(parts):
         for group in range(groups):
             first = (part * groups + group) * WIDE
             down, across = cosine_rows(table_ref[...], numbers_ref[part, group : group + 1, :])
             values_ref[part, group : group + 1, :] = picked(grads_ref[:, first : first + WIDE], down, across)
-
-
-def own_kernel(table_ref, momentum_ref, numbers_ref, own_ref):
-    for group in range(numbers_ref.shape[0]):
-        columns = slice(group * WIDE, (group + 1) * WIDE)
-        down, across = cosine_rows(table_ref[...], numbers_ref[group : group + 1, :])
-        high, low = halves(momentum_ref[:, columns])
+    for group in range(groups):
+        down, across = cosine_rows(table_ref[...], own_numbers_ref[group : group + 1, :])
+        high, low = halves(momentum_ref[:, group * WIDE : (group + 1) * WIDE])
         own_ref[group : group + 1, :] = BETA_DECAY * (picked(high, down, across) + picked(low, down, across))
 
 
-def pick_own(momentum, numbers):
-    return pl.pallas_call(
-        own_kernel,
-        out_shape=jax.ShapeDtypeStruct(numbers.shape, F32),
-        cost_estimate=pl.CostEstimate(flops=4 * 10**8, bytes_accessed=2**19, transcendentals=0),
-        compiler_params=pltpu.CompilerParams(vmem_limit_bytes=32 * 2**20),
-        name="pick_own",
-    )(jnp.asarray(pick_table()), momentum, numbers)
-
-
-def pick(grads, numbers):
+def pick(grads, numbers, momentum, own_numbers):
     return pl.pallas_call(
         pick_kernel,
-        out_shape=jax.ShapeDtypeStruct(numbers.shape, F32),
+        out_shape=[jax.ShapeDtypeStruct(numbers.shape, F32), jax.ShapeDtypeStruct(own_numbers.shape, F32)],
         cost_estimate=pl.CostEstimate(flops=2 * 10**9, bytes_accessed=2**21, transcendentals=0),
         compiler_params=pltpu.CompilerParams(vmem_limit_bytes=16 * 2**20),
         name="pick",
-    )(jnp.asarray(pick_table()), grads, numbers)
+    )(jnp.asarray(pick_table()), grads, numbers, momentum, own_numbers)
 
 
 def block_of(grads_ref, chip, core, step, parts, columns):
@@ -213,15 +199,15 @@
     return total[:TILE] + total[TILE:]
 
 
-def dense_group(sent_ref, rows_ref, group, firsts, replicas):
+def dense_group(sent_ref, rows_ref, group, groups, firsts, replicas):
     count = replicas // GROUP
     for run, first in enumerate(firsts):
 
         def rows(offset):
-            starts = [first + part * SLAB + offset for part in range(GROUP)]
-            return by_tile([sent_ref[pl.ds(start, count, stride=GROUP * SLAB), :] for start in starts])
-
-        values, numbers = rows(group), rows(SLAB // 2 + group)
+            starts = [first + part * 2 * groups + offset for part in range(GROUP)]
+            return by_tile([sent_ref[pl.ds(start, count, stride=GROUP * 2 * groups), :] for start in starts])
+
+        values, numbers = rows(group), rows(groups + group)
         for tile in range(GROUP):
             for part, value in enumerate(parts_of(numbers[tile], values[tile])):
                 rows_ref[group % 2, tile, part, run * count : (run + 1) * count, :] = value
@@ -230,9 +216,10 @@
 
 
 def near_kernel(sent_ref, dense_ref, rows_ref):
-    for group in range(dense_ref.shape[1] // WIDE):
+    groups = dense_ref.shape[1] // WIDE
+    for group in range(groups):
         columns = slice(group * WIDE, (group + 1) * WIDE)
-        dense_ref[:, columns] = dense_group(sent_ref, rows_ref, group, [0], sent_ref.shape[0] // SLAB)
+        dense_ref[:, columns] = dense_group(sent_ref, rows_ref, group, groups, [0], sent_ref.shape[0] // (2 * groups))
 
 
 def near(sent, columns):
@@ -248,11 +235,12 @@
 
 def spread_kernel(at_ref, tall_ref, wide_ref, sent_ref, near_ref, update_ref, rows_ref):
     length = sent_ref.shape[0] // FAR_RUNS
-    firsts = [pl.multiple_of(lax.rem(at_ref[0] + step, FAR_RUNS) * length, SLAB) for step in range(1, FAR_RUNS)]
+    groups = near_ref.shape[1] // WIDE
+    firsts = [pl.multiple_of(lax.rem(at_ref[0] + step, FAR_RUNS) * length, 8) for step in range(1, FAR_RUNS)]
     dense = []
-    for group in range(near_ref.shape[1] // WIDE):
+    for group in range(groups):
         columns = slice(group * WIDE, (group + 1) * WIDE)
-        dense.append(near_ref[:, columns] + dense_group(sent_ref, rows_ref, group, firsts, length // SLAB))
+        dense.append(near_ref[:, columns] + dense_group(sent_ref, rows_ref, group, groups, firsts, length // (2 * groups)))
     for group, piece in enumerate(back(dense, tall_ref[...], wide_ref[...])):
         update_ref[:, group * WIDE : (group + 1) * WIDE] = piece
 
@@ -310,24 +298,21 @@
     own_numbers = indices.reshape(groups, LANES)
     numbers = copies_to(own_numbers, FSDP)
     other = widen(at, grads, chips)
-    own_part = pick_own(momentum, own_numbers)
-    numbers, other, own_part = lax.optimization_barrier((numbers, other, own_part))
+    numbers, other = lax.optimization_barrier((numbers, other))
     arrived = lax.ppermute(other, "core", [(0, 1), (1, 0)])
-    values = pick(grads, numbers)
+    values, own_part = pick(grads, numbers, momentum, own_numbers)
     values = lax.all_to_all(values, FSDP, 0, 0, tiled=True)
     chip_sums = add_own(at, grads, arrived)
     values, chip_sums = lax.optimization_barrier((values, chip_sums))
     selected = jnp.sum(values, axis=0) + own_part
-    own = jnp.concatenate(
-        [jnp.pad(part, ((0, SLAB // 2 - groups), (0, 0))) for part in (selected, own_numbers.astype(F32))], 0
-    )
+    own = jnp.concatenate([selected, own_numbers.astype(F32)], 0).reshape(1, -1)
     sent = copies_to(own, "z")
     parts = [chip_sums[0]]
     for step in (2, 1, 3):
         parts.append(lax.ppermute(chip_sums[step], "x", [(i, (i + step) % chips) for i in range(chips)]))
     left = shared(selected, own_numbers, momentum)
     sent, left = lax.optimization_barrier((sent, left))
-    far = copies_to(sent, "y")
+    far = copies_to(sent.reshape(1, -1), "y")
     dense = near(sent, momentum.shape[1])
     far, dense = lax.optimization_barrier((far, dense))
     update = spread(lax.axis_index("y").astype(jnp.int32)[None], far, dense)

time: 76.4 us -> 76.3 us (level)
  starting transfers between devices: 41.7 us -> 40.6 us
  waiting for transfers between devices: 10.3 us -> 11.3 us
    all_to_all x1, starting transfers between devices: 4.66 us -> 3.28 us  [on_device(): values = lax.all_to_all(values, FSDP, 0, 0, tiled=True)]
    all_to_all x3, waiting for transfers between devices: 1.2 us -> 2.3 us  [copies_to(): lax.all_to_all(jnp.broadcast_to(block[None], (count,) + block.shape), axi...]
    pallas_call x2 -> x1, Pallas kernels: 4.7 us -> 4.25 us  [pick(): pl.pallas_call(pick_kernel, out_shape=[jax.ShapeDtypeStruct(numbers.shape...]
  transfers between devices with their start and end apart: 8 -> 8, of which waited for: 3 -> 4; matrix products, arithmetic and copies ran while one was open for 4% -> 4% of each run, Pallas kernels for 12% -> 12%
where the time goes in v5:
time: 76.3 us; the launch traced here: 75.6 us
  starting transfers between devices  40.6 us (53%)
  Pallas kernels  13.2 us (17%)
  waiting for transfers between devices  11.3 us (15%)
  local copies, waits for them, and re-layouts  6.74 us (9%)
  other arithmetic  2.9 us (4%)
  between operations  0.82 us (1%)
    all_to_all x3, starting transfers between devices, copies_to(): lax.all_to_all(jnp.broadcast_to(block[None], (count,) + block.shape), axi...  24.8 us
    ppermute x3, starting transfers between devices, on_device(): lax.ppermute(chip_sums[step], 'x', [(i, (i + step) % chips) for i in rang...  9.88 us
    ppermute x3, waiting for transfers between devices, on_device(): lax.ppermute(chip_sums[step], 'x', [(i, (i + step) % chips) for i in rang...  7.64 us
    pallas_call x1, Pallas kernels, spread(): pl.pallas_call(spread_kernel, in_specs=[pl.BlockSpec(memory_space=pltpu.S...  4.4 us
    unnamed x18, local copies, waits for them, and re-layouts  4.31 us
    pallas_call x1, Pallas kernels, pick(): pl.pallas_call(pick_kernel, out_shape=[jax.ShapeDtypeStruct(numbers.shape...  4.25 us
    all_to_all x1, starting transfers between devices, on_device(): values = lax.all_to_all(values, FSDP, 0, 0, tiled=True)  3.28 us
    ppermute x1, starting transfers between devices, on_device(): arrived = lax.ppermute(other, 'core', [(0, 1), (1, 0)])  2.63 us
  transfers between devices with their start and end apart: 8, of which 4 were waited for; matrix products, arithmetic and copies ran while one was open for 4% of the time, Pallas kernels for 12%

profile of v5, /device:TPU:1, one launch (start us, length us, event | category | flops | bytes accessed | tf_op | source)
XLA Modules:
  0.0 75.6 jit_solution(5049766956735966369)
XLA Ops:
  0.6 0.8 reduce
  2.1 10.1 %all-to-all-start = ((s32[8,7,128]{2,1,0:T(8,128)}), s32[8,7,128]{2,1,0:T(8,128)S(1)}, u32[]{:S(2)}, u32[]{:S(2)}) async-start(s32[8,7,128]{2,1,0:T(8,128)} %broadcast_in_dim.28), calls=%async_computation | async-start | bytes 65536 | tf_op jit(solution)/shard_map/all_to_all | solution.py:290
  12.3 1.5 %copy-done = bf16[1,1,64,14336]{3,2,1,0:T(8,128)(2,1)S(1)} copy-done((bf16[1,1,64,14336]{3,2,1,0:T(8,128)(2,1)S(1)}, bf16[1,1,64,14336]{3,2,1,0:T(8,128)(2,1)}, u32[]{:S(2)}) %copy-start) | copy-done | bytes 1835032
  14.5 1.3 %copy-done.2 = f32[4,64,1792]{2,1,0:T(8,128)} copy-done((f32[4,64,1792]{2,1,0:T(8,128)}, f32[4,64,1792]{2,1,0:T(8,128)S(1)}, u32[]{:S(2)}) %copy-start.2) | copy-done | bytes 1835032
  15.7 1.2 %all-to-all-done.numbers_ref = s32[8,7,128]{2,1,0:T(8,128)S(1)} async-done(((s32[8,7,128]{2,1,0:T(8,128)}), s32[8,7,128]{2,1,0:T(8,128)S(1)}, u32[]{:S(2)}, u32[]{:S(2)}) %all-to-all-start) | async-done | bytes 28704 | tf_op jit(solution)/shard_map/all_to_all | solution.py:290
  16.9 2.6 %collective-permute-start = (f32[4,64,1792]{2,1,0:T(8,128)}, f32[4,64,1792]{2,1,0:T(8,128)}, u32[]{:S(2)}, u32[]{:S(2)}) collective-permute-start(f32[4,64,1792]{2,1,0:T(8,128)} %copy-done.2), channel_id=1, source_target_pairs={{0,1},{1,0},{2,3},{3,2},{4,5},{5,4},{6,7},{7,6},{8,9},{9,8},{10,11... | collective-permute-start | bytes 5505032 | tf_op jit(solution)/shard_map/ppermute | solution.py:302
  19.6 4.2 %pick.1 = (f32[8,7,128]{2,1,0:T(8,128)}, f32[7,128]{1,0:T(8,128)S(1)}) custom-call(bf16[256,128]{1,0:T(8,128)(2,1)S(1)} %copy-done.7, bf16[64,14336]{1,0:T(8,128)(2,1)S(1)} %bitcast.13, s32[8,7,128]{2,1,0:T(8,128)S(1)} %all-to-all-done.numbers_ref, f32[64,1792]{1,0:T(8,128)S(1)} %bitcast.18, s32[7,128]{1,0:T(8,128)S(1)} %broadcast_in_dim.27.own_numbers_ref.numbers_ref), custom_call_target="tpu_custom_call" | custom-call | flops 2000000000 | bytes 2097152 | tf_op jit(solution)/shard_map/pick/pallas_call | solution.py:93
  23.9 3.3 %all-to-all-start.1 = ((f32[8,7,128]{2,1,0:T(8,128)}), f32[8,7,128]{2,1,0:T(8,128)S(1)}, u32[]{:S(2)}, u32[]{:S(2)}) async-start(f32[8,7,128]{2,1,0:T(8,128)} %get-tuple-element.20), calls=%async_computation.1 | async-start | bytes 65536 | tf_op jit(solution)/shard_map/all_to_all | solution.py:304
  27.2 1.7 %add_own.1 = (f32[64,1792]{1,0:T(8,128)S(1)}, f32[64,1792]{1,0:T(8,128)S(1)}, f32[64,1792]{1,0:T(8,128)S(1)}, f32[64,1792]{1,0:T(8,128)S(1)}) custom-call(s32[2]{0:T(128)S(1)} %pad_add_fusion.at_ref, bf16[64,14336]{1,0:T(8,128)(2,1)S(1)} %bitcast.14, f32[4,64,1792]{2,1,0:T(8,128)} %collective-permute-done.arrived_ref), custom_call_target="tpu_custom_call" | custom-call | flops 1000000 | bytes 5242880 | tf_op jit(solution)/shard_map/add_own/pallas_call | solution.py:134
  28.9 0.8 %copy-done.4 = f32[64,1792]{1,0:T(8,128)} copy-done((f32[64,1792]{1,0:T(8,128)}, f32[64,1792]{1,0:T(8,128)S(1)}, u32[]{:S(2)}) %copy-start.4) | copy-done | bytes 458776
  29.7 0.8 %copy-done.5 = f32[64,1792]{1,0:T(8,128)} copy-done((f32[64,1792]{1,0:T(8,128)}, f32[64,1792]{1,0:T(8,128)S(1)}, u32[]{:S(2)}) %copy-start.5) | copy-done | bytes 458776
  30.5 1.4 %all-to-all-done.1 = f32[8,7,128]{2,1,0:T(8,128)S(1)} async-done(((f32[8,7,128]{2,1,0:T(8,128)}), f32[8,7,128]{2,1,0:T(8,128)S(1)}, u32[]{:S(2)}, u32[]{:S(2)}) %all-to-all-start.1) | async-done | bytes 28704 | tf_op jit(solution)/shard_map/all_to_all | solution.py:304
  32.6 10.6 %all-to-all-start.2 = ((f32[16,1,1792]{2,1,0:T(1,128)}), f32[16,1,1792]{2,1,0:T(1,128)S(1)}, u32[]{:S(2)}, u32[]{:S(2)}) async-start(f32[16,1,1792]{2,1,0:T(1,128)} %broadcast_in_dim.30), calls=%async_computation.2 | async-start | bytes 229376 | tf_op jit(solution)/shard_map/all_to_all | solution.py:290
  43.2 3.4 %collective-permute-start.1 = (f32[64,1792]{1,0:T(8,128)}, f32[64,1792]{1,0:T(8,128)S(1)}, u32[]{:S(2)}, u32[]{:S(2)}) collective-permute-start(f32[64,1792]{1,0:T(8,128)} %copy-done.5), channel_id=1, source_target_pairs={{0,4},{2,6},{4,0},{6,2},{1,5},{3,7},{5,1},{7,3},{8,12},{10,14},{12... | collective-permute-start | bytes 1376264 | tf_op jit(solution)/shard_map/ppermute | solution.py:312
  46.6 2.2 %collective-permute-start.2 = (f32[64,1792]{1,0:T(8,128)}, f32[64,1792]{1,0:T(8,128)}, u32[]{:S(2)}, u32[]{:S(2)}) collective-permute-start(f32[64,1792]{1,0:T(8,128)} %copy-done.4), channel_id=1, source_target_pairs={{0,2},{2,4},{4,6},{6,0},{1,3},{3,5},{5,7},{7,1},{8,10},{10,12},{12... | collective-permute-start | bytes 1376264 | tf_op jit(solution)/shard_map/ppermute | solution.py:312
  48.8 4.3 %collective-permute-start.3 = (f32[64,1792]{1,0:T(8,128)S(1)}, f32[64,1792]{1,0:T(8,128)}, u32[]{:S(2)}, u32[]{:S(2)}) collective-permute-start(f32[64,1792]{1,0:T(8,128)S(1)} %get-tuple-element.32), channel_id=1, source_target_pairs={{0,6},{2,0},{4,2},{6,4},{1,7},{3,1},{5,3},{7,5},{8,14},{10,8},{12,... | collective-permute-start | bytes 1376264 | tf_op jit(solution)/shard_map/ppermute | solution.py:312
  53.1 0.9 %shared.1 = f32[64,1792]{1,0:T(8,128)S(1)} custom-call(bf16[64,192]{1,0:T(8,128)(2,1)S(1)} %copy-done.8, bf16[512,256]{1,0:T(8,128)(2,1)S(1)} %copy-done.6, f32[7,128]{1,0:T(8,128)S(1)} %add.15.values_ref, s32[7,128]{1,0:T(8,128)S(1)} %broadcast_in_dim.27.own_numbers_ref.numbers_ref, f32[64,1792]{1,0:T(8,128)S(1)} %bitcast.19), custom_call_target="tpu_custom_call" | custom-call | flops 400000000 | bytes 1048576 | tf_op jit(solution)/shard_map/shared/pallas_call | solution.py:276
  54.0 1.1 %all-to-all-done.2 = f32[16,1,1792]{2,1,0:T(1,128)S(1)} async-done(((f32[16,1,1792]{2,1,0:T(1,128)}), f32[16,1,1792]{2,1,0:T(1,128)S(1)}, u32[]{:S(2)}, u32[]{:S(2)}) %all-to-all-start.2) | async-done | bytes 114720 | tf_op jit(solution)/shard_map/all_to_all | solution.py:290
  55.1 1.0 %broadcast_in_dim.34 = f32[4,1,28672]{2,1,0:T(1,128)} broadcast(f32[28672]{0:T(1024)S(1)} %bitcast.16), dimensions={2} | broadcast | bytes 573440 | tf_op jit(solution)/shard_map/broadcast_in_dim | solution.py:290
  56.1 4.2 %all-to-all-start.3 = ((f32[4,1,28672]{2,1,0:T(1,128)}), f32[4,1,28672]{2,1,0:T(1,128)S(1)}, u32[]{:S(2)}, u32[]{:S(2)}) async-start(f32[4,1,28672]{2,1,0:T(1,128)} %broadcast_in_dim.34), calls=%async_computation.3 | async-start | bytes 917504 | tf_op jit(solution)/shard_map/all_to_all | solution.py:290
  60.3 1.3 %near.1.near_ref = f32[64,1792]{1,0:T(8,128)S(1)} custom-call(f32[224,128]{1,0:T(8,128)S(1)} %bitcast.17), custom_call_target="tpu_custom_call" | custom-call | flops 1000000000 | bytes 1048576 | tf_op jit(solution)/shard_map/near/pallas_call | solution.py:226
  61.6 7.6 %collective-permute-done.2 = f32[64,1792]{1,0:T(8,128)} collective-permute-done((f32[64,1792]{1,0:T(8,128)}, f32[64,1792]{1,0:T(8,128)}, u32[]{:S(2)}, u32[]{:S(2)}) %collective-permute-start.2) | collective-permute-done | bytes 458784 | tf_op jit(solution)/shard_map/ppermute | solution.py:312
  69.2 2.0 %add_bitcast_fusion = f32[1,64,1792]{2,1,0:T(8,128)} fusion(f32[64,1792]{1,0:T(8,128)S(1)} %shared.1, f32[64,1792]{1,0:T(8,128)} %collective-permute-done.3, f32[64,1792]{1,0:T(8,128)} %collective-permute-done.2, f32[64,1792]{1,0:T(8,128)S(1)} %get-tuple-element.29, f32[64,1792]{1,0:T(8,128)S(1)} %collective-permute-done.1), kind=kLoop, calls=%fused_computation | loop fusion | flops 458752 | bytes 2752512 | tf_op jit(solution)/shard_map/broadcast_in_dim | solution.py:319
  71.2 4.4 %spread.1 = f32[64,1792]{1,0:T(8,128)} custom-call(s32[1]{0:T(128)} %bitcast.6.at_ref, bf16[64,192]{1,0:T(8,128)(2,1)S(1)} %copy-done.8, bf16[512,256]{1,0:T(8,128)(2,1)S(1)} %copy-done.6, f32[896,128]{1,0:T(8,128)S(1)} %bitcast.15, f32[64,1792]{1,0:T(8,128)S(1)} %near.1.near_ref), custom_call_target="tpu_custom_call" | custom-call | flops 2000000000 | bytes 1048576 | tf_op jit(solution)/shard_map/spread/pallas_call | solution.py:250
  (27 shorter events, 2.2 us)
Async XLA Ops:
  2.1 14.9 %all-to-all-start = ((s32[8,7,128]{2,1,0:T(8,128)}), s32[8,7,128]{2,1,0:T(8,128)S(1)}, u32[]{:S(2)}, u32[]{:S(2)}) async-start(s32[8,7,128]{2,1,0:T(8,128)} %broadcast_in_dim.28), calls=%async_computation | async-start | bytes 65536 | tf_op jit(solution)/shard_map/all_to_all | solution.py:290
  12.3 1.5 %copy-start = (bf16[1,1,64,14336]{3,2,1,0:T(8,128)(2,1)S(1)}, bf16[1,1,64,14336]{3,2,1,0:T(8,128)(2,1)}, u32[]{:S(2)}) copy-start(bf16[1,1,64,14336]{3,2,1,0:T(8,128)(2,1)} %param.8) | copy-start | bytes 5505028
  13.8 5.8 %copy-start.1 = (bf16[1,1,64,14336]{3,2,1,0:T(8,128)(2,1)S(1)}, bf16[1,1,64,14336]{3,2,1,0:T(8,128)(2,1)}, u32[]{:S(2)}) copy-start(bf16[1,1,64,14336]{3,2,1,0:T(8,128)(2,1)} %param.8) | copy-start | bytes 5505028
  13.8 5.8 %copy-start.3 = (f32[1,64,1792]{2,1,0:T(8,128)S(1)}, f32[1,64,1792]{2,1,0:T(8,128)}, u32[]{:S(2)}) copy-start(f32[1,64,1792]{2,1,0:T(8,128)} %param.9) | copy-start | bytes 1376260
  13.8 5.8 %copy-start.7 = (bf16[256,128]{1,0:T(8,128)(2,1)S(1)}, bf16[256,128]{1,0:T(8,128)(2,1)}, u32[]{:S(2)}) copy-start(bf16[256,128]{1,0:T(8,128)(2,1)} %constant.20.clone.table_ref) | copy-start | bytes 196612
  14.5 1.3 %copy-start.2 = (f32[4,64,1792]{2,1,0:T(8,128)}, f32[4,64,1792]{2,1,0:T(8,128)S(1)}, u32[]{:S(2)}) copy-start(f32[4,64,1792]{2,1,0:T(8,128)S(1)} %widen.1) | copy-start | bytes 5505028
  16.9 10.2 %collective-permute-start = (f32[4,64,1792]{2,1,0:T(8,128)}, f32[4,64,1792]{2,1,0:T(8,128)}, u32[]{:S(2)}, u32[]{:S(2)}) collective-permute-start(f32[4,64,1792]{2,1,0:T(8,128)} %copy-done.2), channel_id=1, source_target_pairs={{0,1},{1,0},{2,3},{3,2},{4,5},{5,4},{6,7},{7,6},{8,9},{9,8},{10,11... | collective-permute-start | bytes 5505032 | tf_op jit(solution)/shard_map/ppermute | solution.py:302
  23.9 8.0 %all-to-all-start.1 = ((f32[8,7,128]{2,1,0:T(8,128)}), f32[8,7,128]{2,1,0:T(8,128)S(1)}, u32[]{:S(2)}, u32[]{:S(2)}) async-start(f32[8,7,128]{2,1,0:T(8,128)} %get-tuple-element.20), calls=%async_computation.1 | async-start | bytes 65536 | tf_op jit(solution)/shard_map/all_to_all | solution.py:304
  27.2 26.0 %copy-start.6 = (bf16[512,256]{1,0:T(8,128)(2,1)S(1)}, bf16[512,256]{1,0:T(8,128)(2,1)}, u32[]{:S(2)}) copy-start(bf16[512,256]{1,0:T(8,128)(2,1)} %constant.22.clone.wide_ref) | copy-start | bytes 786436
  27.2 26.0 %copy-start.8 = (bf16[64,192]{1,0:T(8,128)(2,1)S(1)}, bf16[64,192]{1,0:T(8,128)(2,1)}, u32[]{:S(2)}) copy-start(bf16[64,192]{1,0:T(8,128)(2,1)} %constant.21.clone.tall_ref) | copy-start | bytes 73732
  28.9 0.8 %copy-start.4 = (f32[64,1792]{1,0:T(8,128)}, f32[64,1792]{1,0:T(8,128)S(1)}, u32[]{:S(2)}) copy-start(f32[64,1792]{1,0:T(8,128)S(1)} %get-tuple-element.31) | copy-start | bytes 1376260
  29.7 0.8 %copy-start.5 = (f32[64,1792]{1,0:T(8,128)}, f32[64,1792]{1,0:T(8,128)S(1)}, u32[]{:S(2)}) copy-start(f32[64,1792]{1,0:T(8,128)S(1)} %get-tuple-element.30) | copy-start | bytes 1376260
  32.6 22.5 %all-to-all-start.2 = ((f32[16,1,1792]{2,1,0:T(1,128)}), f32[16,1,1792]{2,1,0:T(1,128)S(1)}, u32[]{:S(2)}, u32[]{:S(2)}) async-start(f32[16,1,1792]{2,1,0:T(1,128)} %broadcast_in_dim.30), calls=%async_computation.2 | async-start | bytes 229376 | tf_op jit(solution)/shard_map/all_to_all | solution.py:290
  43.2 18.3 %collective-permute-start.1 = (f32[64,1792]{1,0:T(8,128)}, f32[64,1792]{1,0:T(8,128)S(1)}, u32[]{:S(2)}, u32[]{:S(2)}) collective-permute-start(f32[64,1792]{1,0:T(8,128)} %copy-done.5), channel_id=1, source_target_pairs={{0,4},{2,6},{4,0},{6,2},{1,5},{3,7},{5,1},{7,3},{8,12},{10,14},{12... | collective-permute-start | bytes 1376264 | tf_op jit(solution)/shard_map/ppermute | solution.py:312
  46.6 22.6 %collective-permute-start.2 = (f32[64,1792]{1,0:T(8,128)}, f32[64,1792]{1,0:T(8,128)}, u32[]{:S(2)}, u32[]{:S(2)}) collective-permute-start(f32[64,1792]{1,0:T(8,128)} %copy-done.4), channel_id=1, source_target_pairs={{0,2},{2,4},{4,6},{6,0},{1,3},{3,5},{5,7},{7,1},{8,10},{10,12},{12... | collective-permute-start | bytes 1376264 | tf_op jit(solution)/shard_map/ppermute | solution.py:312
  48.8 20.4 %collective-permute-start.3 = (f32[64,1792]{1,0:T(8,128)S(1)}, f32[64,1792]{1,0:T(8,128)}, u32[]{:S(2)}, u32[]{:S(2)}) collective-permute-start(f32[64,1792]{1,0:T(8,128)S(1)} %get-tuple-element.32), channel_id=1, source_target_pairs={{0,6},{2,0},{4,2},{6,4},{1,7},{3,1},{5,3},{7,5},{8,14},{10,8},{12,... | collective-permute-start | bytes 1376264 | tf_op jit(solution)/shard_map/ppermute | solution.py:312
  56.1 15.1 %all-to-all-start.3 = ((f32[4,1,28672]{2,1,0:T(1,128)}), f32[4,1,28672]{2,1,0:T(1,128)S(1)}, u32[]{:S(2)}, u32[]{:S(2)}) async-start(f32[4,1,28672]{2,1,0:T(1,128)} %broadcast_in_dim.34), calls=%async_computation.3 | async-start | bytes 917504 | tf_op jit(solution)/shard_map/all_to_all | solution.py:290

commit v6 on v5

--- a/solution.py
+++ b/solution.py
@@ -310,8 +310,9 @@
     parts = [chip_sums[0]]
     for step in (2, 1, 3):
         parts.append(lax.ppermute(chip_sums[step], "x", [(i, (i + step) % chips) for i in range(chips)]))
-    left = shared(selected, own_numbers, momentum)
-    sent, left = lax.optimization_barrier((sent, left))
+    chosen = (own.reshape(-1, LANES)[groups:]).astype(jnp.int32)
+    sent, chosen = lax.optimization_barrier((sent, chosen))
+    left = shared(selected, chosen, momentum)
     far = copies_to(sent.reshape(1, -1), "y")
     dense = near(sent, momentum.shape[1])
     far, dense = lax.optimization_barrier((far, dense))

time: 76.3 us -> 76 us (level)
    ppermute x3, waiting for transfers between devices: 7.64 us -> 6.67 us  [on_device(): lax.ppermute(chip_sums[step], 'x', [(i, (i + step) % chips) for i in rang...]
    all_to_all x3, waiting for transfers between devices: 2.3 us -> 3.26 us  [copies_to(): lax.all_to_all(jnp.broadcast_to(block[None], (count,) + block.shape), axi...]
where the time goes in v6:
time: 76 us; the launch traced here: 75.4 us
  starting transfers between devices  40.6 us (53%)
  Pallas kernels  13.2 us (17%)
  waiting for transfers between devices  11.4 us (15%)
  local copies, waits for them, and re-layouts  6.68 us (9%)
  other arithmetic  2.8 us (4%)
  between operations  0.79 us (1%)
    all_to_all x3, starting transfers between devices, copies_to(): lax.all_to_all(jnp.broadcast_to(block[None], (count,) + block.shape), axi...  24.9 us
    ppermute x3, starting transfers between devices, on_device(): lax.ppermute(chip_sums[step], 'x', [(i, (i + step) % chips) for i in rang...  9.83 us
    ppermute x3, waiting for transfers between devices, on_device(): lax.ppermute(chip_sums[step], 'x', [(i, (i + step) % chips) for i in rang...  6.67 us
    pallas_call x1, Pallas kernels, spread(): pl.pallas_call(spread_kernel, in_specs=[pl.BlockSpec(memory_space=pltpu.S...  4.41 us
    unnamed x18, local copies, waits for them, and re-layouts  4.3 us
    pallas_call x1, Pallas kernels, pick(): pl.pallas_call(pick_kernel, out_shape=[jax.ShapeDtypeStruct(numbers.shape...  4.27 us
    all_to_all x1, starting transfers between devices, on_device(): values = lax.all_to_all(values, FSDP, 0, 0, tiled=True)  3.28 us
    all_to_all x3, waiting for transfers between devices, copies_to(): lax.all_to_all(jnp.broadcast_to(block[None], (count,) + block.shape), axi...  3.26 us
  transfers between devices with their start and end apart: 8, of which 4 were waited for; matrix products, arithmetic and copies ran while one was open for 4% of the time, Pallas kernels for 12%

profile of v6, /device:TPU:1, one launch (start us, length us, event | category | flops | bytes accessed | tf_op | source)
XLA Modules:
  0.0 75.4 jit_solution(14914546696160378844)
XLA Ops:
  0.6 0.8 %reduce = s32[28,32]{1,0:T(8,128)S(1)} reduce(s32[1,1,28,32]{3,1,2,0:T(1,128)} %param.10, s32[]{:T(128)} %constant.26), dimensions={0,1}, to_apply=%param.10.reduce_sub_computation | reduce | bytes 7172 | tf_op args[2]
  2.1 10.1 %all-to-all-start = ((s32[8,7,128]{2,1,0:T(8,128)}), s32[8,7,128]{2,1,0:T(8,128)S(1)}, u32[]{:S(2)}, u32[]{:S(2)}) async-start(s32[8,7,128]{2,1,0:T(8,128)} %broadcast_in_dim.28), calls=%async_computation | async-start | bytes 65536 | tf_op jit(solution)/shard_map/all_to_all | solution.py:290
  12.3 1.5 %copy-done = bf16[1,1,64,14336]{3,2,1,0:T(8,128)(2,1)S(1)} copy-done((bf16[1,1,64,14336]{3,2,1,0:T(8,128)(2,1)S(1)}, bf16[1,1,64,14336]{3,2,1,0:T(8,128)(2,1)}, u32[]{:S(2)}) %copy-start) | copy-done | bytes 1835032
  14.5 1.2 %copy-done.2 = f32[4,64,1792]{2,1,0:T(8,128)} copy-done((f32[4,64,1792]{2,1,0:T(8,128)}, f32[4,64,1792]{2,1,0:T(8,128)S(1)}, u32[]{:S(2)}) %copy-start.2) | copy-done | bytes 1835032
  15.7 1.2 %all-to-all-done.numbers_ref = s32[8,7,128]{2,1,0:T(8,128)S(1)} async-done(((s32[8,7,128]{2,1,0:T(8,128)}), s32[8,7,128]{2,1,0:T(8,128)S(1)}, u32[]{:S(2)}, u32[]{:S(2)}) %all-to-all-start) | async-done | bytes 28704 | tf_op jit(solution)/shard_map/all_to_all | solution.py:290
  16.9 2.6 %collective-permute-start = (f32[4,64,1792]{2,1,0:T(8,128)}, f32[4,64,1792]{2,1,0:T(8,128)}, u32[]{:S(2)}, u32[]{:S(2)}) collective-permute-start(f32[4,64,1792]{2,1,0:T(8,128)} %copy-done.2), channel_id=1, source_target_pairs={{0,1},{1,0},{2,3},{3,2},{4,5},{5,4},{6,7},{7,6},{8,9},{9,8},{10,11... | collective-permute-start | bytes 5505032 | tf_op jit(solution)/shard_map/ppermute | solution.py:302
  19.6 4.3 %pick.1 = (f32[8,7,128]{2,1,0:T(8,128)}, f32[7,128]{1,0:T(8,128)S(1)}) custom-call(bf16[256,128]{1,0:T(8,128)(2,1)S(1)} %copy-done.7, bf16[64,14336]{1,0:T(8,128)(2,1)S(1)} %bitcast.13, s32[8,7,128]{2,1,0:T(8,128)S(1)} %all-to-all-done.numbers_ref, f32[64,1792]{1,0:T(8,128)S(1)} %bitcast.18, s32[7,128]{1,0:T(8,128)S(1)} %broadcast_in_dim.27.own_numbers_ref), custom_call_target="tpu_custom_call" | custom-call | flops 2000000000 | bytes 2097152 | tf_op jit(solution)/shard_map/pick/pallas_call | solution.py:93
  23.9 3.3 %all-to-all-start.1 = ((f32[8,7,128]{2,1,0:T(8,128)}), f32[8,7,128]{2,1,0:T(8,128)S(1)}, u32[]{:S(2)}, u32[]{:S(2)}) async-start(f32[8,7,128]{2,1,0:T(8,128)} %get-tuple-element.20), calls=%async_computation.1 | async-start | bytes 65536 | tf_op jit(solution)/shard_map/all_to_all | solution.py:304
  27.2 1.7 %add_own.1 = (f32[64,1792]{1,0:T(8,128)S(1)}, f32[64,1792]{1,0:T(8,128)S(1)}, f32[64,1792]{1,0:T(8,128)S(1)}, f32[64,1792]{1,0:T(8,128)S(1)}) custom-call(s32[2]{0:T(128)S(1)} %pad_add_fusion.at_ref, bf16[64,14336]{1,0:T(8,128)(2,1)S(1)} %bitcast.14, f32[4,64,1792]{2,1,0:T(8,128)} %collective-permute-done.arrived_ref), custom_call_target="tpu_custom_call" | custom-call | flops 1000000 | bytes 5242880 | tf_op jit(solution)/shard_map/add_own/pallas_call | solution.py:134
  28.9 0.8 %copy-done.4 = f32[64,1792]{1,0:T(8,128)} copy-done((f32[64,1792]{1,0:T(8,128)}, f32[64,1792]{1,0:T(8,128)S(1)}, u32[]{:S(2)}) %copy-start.4) | copy-done | bytes 458776
  29.7 0.8 %copy-done.5 = f32[64,1792]{1,0:T(8,128)} copy-done((f32[64,1792]{1,0:T(8,128)}, f32[64,1792]{1,0:T(8,128)S(1)}, u32[]{:S(2)}) %copy-start.5) | copy-done | bytes 458776
  30.4 1.4 %all-to-all-done.1 = f32[8,7,128]{2,1,0:T(8,128)S(1)} async-done(((f32[8,7,128]{2,1,0:T(8,128)}), f32[8,7,128]{2,1,0:T(8,128)S(1)}, u32[]{:S(2)}, u32[]{:S(2)}) %all-to-all-start.1) | async-done | bytes 28704 | tf_op jit(solution)/shard_map/all_to_all | solution.py:304
  32.6 10.6 %all-to-all-start.2 = ((f32[16,1,1792]{2,1,0:T(1,128)}), f32[16,1,1792]{2,1,0:T(1,128)S(1)}, u32[]{:S(2)}, u32[]{:S(2)}) async-start(f32[16,1,1792]{2,1,0:T(1,128)} %broadcast_in_dim.30), calls=%async_computation.2 | async-start | bytes 229376 | tf_op jit(solution)/shard_map/all_to_all | solution.py:290
  43.2 3.3 %collective-permute-start.1 = (f32[64,1792]{1,0:T(8,128)}, f32[64,1792]{1,0:T(8,128)S(1)}, u32[]{:S(2)}, u32[]{:S(2)}) collective-permute-start(f32[64,1792]{1,0:T(8,128)} %copy-done.5), channel_id=1, source_target_pairs={{0,4},{2,6},{4,0},{6,2},{1,5},{3,7},{5,1},{7,3},{8,12},{10,14},{12... | collective-permute-start | bytes 1376264 | tf_op jit(solution)/shard_map/ppermute | solution.py:312
  46.5 2.2 %collective-permute-start.2 = (f32[64,1792]{1,0:T(8,128)}, f32[64,1792]{1,0:T(8,128)S(1)}, u32[]{:S(2)}, u32[]{:S(2)}) collective-permute-start(f32[64,1792]{1,0:T(8,128)} %copy-done.4), channel_id=1, source_target_pairs={{0,2},{2,4},{4,6},{6,0},{1,3},{3,5},{5,7},{7,1},{8,10},{10,12},{12... | collective-permute-start | bytes 1376264 | tf_op jit(solution)/shard_map/ppermute | solution.py:312
  48.8 4.3 %collective-permute-start.3 = (f32[64,1792]{1,0:T(8,128)S(1)}, f32[64,1792]{1,0:T(8,128)}, u32[]{:S(2)}, u32[]{:S(2)}) collective-permute-start(f32[64,1792]{1,0:T(8,128)S(1)} %get-tuple-element.32), channel_id=1, source_target_pairs={{0,6},{2,0},{4,2},{6,4},{1,7},{3,1},{5,3},{7,5},{8,14},{10,8},{12,... | collective-permute-start | bytes 1376264 | tf_op jit(solution)/shard_map/ppermute | solution.py:312
  53.0 2.0 %all-to-all-done.2 = f32[16,1,1792]{2,1,0:T(1,128)S(1)} async-done(((f32[16,1,1792]{2,1,0:T(1,128)}), f32[16,1,1792]{2,1,0:T(1,128)S(1)}, u32[]{:S(2)}, u32[]{:S(2)}) %all-to-all-start.2) | async-done | bytes 114720 | tf_op jit(solution)/shard_map/all_to_all | solution.py:290
  55.1 1.0 %broadcast_in_dim.34 = f32[4,1,28672]{2,1,0:T(1,128)} broadcast(f32[28672]{0:T(1024)S(1)} %bitcast.16), dimensions={2} | broadcast | bytes 573440 | tf_op jit(solution)/shard_map/broadcast_in_dim | solution.py:290
  56.1 4.2 %all-to-all-start.3 = ((f32[4,1,28672]{2,1,0:T(1,128)}), f32[4,1,28672]{2,1,0:T(1,128)S(1)}, u32[]{:S(2)}, u32[]{:S(2)}) async-start(f32[4,1,28672]{2,1,0:T(1,128)} %broadcast_in_dim.34), calls=%async_computation.3 | async-start | bytes 917504 | tf_op jit(solution)/shard_map/all_to_all | solution.py:290
  60.3 0.9 %shared.1 = f32[64,1792]{1,0:T(8,128)S(1)} custom-call(bf16[64,192]{1,0:T(8,128)(2,1)S(1)} %copy-done.8, bf16[512,256]{1,0:T(8,128)(2,1)S(1)} %copy-done.6, f32[7,128]{1,0:T(8,128)S(1)} %add.15.values_ref, s32[7,128]{1,0:T(8,128)S(1)} %get-tuple-element.28.numbers_ref, f32[64,1792]{1,0:T(8,128)S(1)} %bitcast.19), custom_call_target="tpu_custom_call" | custom-call | flops 400000000 | bytes 1048576 | tf_op jit(solution)/shard_map/shared/pallas_call | solution.py:276
  61.1 1.3 %near.1.near_ref = f32[64,1792]{1,0:T(8,128)S(1)} custom-call(f32[224,128]{1,0:T(8,128)S(1)} %bitcast.17), custom_call_target="tpu_custom_call" | custom-call | flops 1000000000 | bytes 1048576 | tf_op jit(solution)/shard_map/near/pallas_call | solution.py:226
  62.4 6.7 %collective-permute-done.2 = f32[64,1792]{1,0:T(8,128)S(1)} collective-permute-done((f32[64,1792]{1,0:T(8,128)}, f32[64,1792]{1,0:T(8,128)S(1)}, u32[]{:S(2)}, u32[]{:S(2)}) %collective-permute-start.2) | collective-permute-done | bytes 458784 | tf_op jit(solution)/shard_map/ppermute | solution.py:312
  69.1 1.9 %add_bitcast_fusion = f32[1,64,1792]{2,1,0:T(8,128)} fusion(f32[64,1792]{1,0:T(8,128)S(1)} %shared.1, f32[64,1792]{1,0:T(8,128)} %collective-permute-done.3, f32[64,1792]{1,0:T(8,128)S(1)} %collective-permute-done.2, f32[64,1792]{1,0:T(8,128)S(1)} %get-tuple-element.29, f32[64,1792]{1,0:T(8,128)S(1)} %collective-permute-done.1), kind=kLoop, calls=%fused_computation | loop fusion | flops 458752 | bytes 2752512 | tf_op jit(solution)/shard_map/broadcast_in_dim | solution.py:320
  71.0 4.4 %spread.1 = f32[64,1792]{1,0:T(8,128)} custom-call(s32[1]{0:T(128)} %bitcast.6.at_ref, bf16[64,192]{1,0:T(8,128)(2,1)S(1)} %copy-done.8, bf16[512,256]{1,0:T(8,128)(2,1)S(1)} %copy-done.6, f32[896,128]{1,0:T(8,128)S(1)} %bitcast.15, f32[64,1792]{1,0:T(8,128)S(1)} %near.1.near_ref), custom_call_target="tpu_custom_call" | custom-call | flops 2000000000 | bytes 1048576 | tf_op jit(solution)/shard_map/spread/pallas_call | solution.py:250
  (27 shorter events, 2.2 us)
Async XLA Ops:
  2.1 14.9 %all-to-all-start = ((s32[8,7,128]{2,1,0:T(8,128)}), s32[8,7,128]{2,1,0:T(8,128)S(1)}, u32[]{:S(2)}, u32[]{:S(2)}) async-start(s32[8,7,128]{2,1,0:T(8,128)} %broadcast_in_dim.28), calls=%async_computation | async-start | bytes 65536 | tf_op jit(solution)/shard_map/all_to_all | solution.py:290
  12.3 1.5 %copy-start = (bf16[1,1,64,14336]{3,2,1,0:T(8,128)(2,1)S(1)}, bf16[1,1,64,14336]{3,2,1,0:T(8,128)(2,1)}, u32[]{:S(2)}) copy-start(bf16[1,1,64,14336]{3,2,1,0:T(8,128)(2,1)} %param.8) | copy-start | bytes 5505028
  13.8 5.8 %copy-start.1 = (bf16[1,1,64,14336]{3,2,1,0:T(8,128)(2,1)S(1)}, bf16[1,1,64,14336]{3,2,1,0:T(8,128)(2,1)}, u32[]{:S(2)}) copy-start(bf16[1,1,64,14336]{3,2,1,0:T(8,128)(2,1)} %param.8) | copy-start | bytes 5505028
  13.8 5.8 %copy-start.3 = (f32[1,64,1792]{2,1,0:T(8,128)S(1)}, f32[1,64,1792]{2,1,0:T(8,128)}, u32[]{:S(2)}) copy-start(f32[1,64,1792]{2,1,0:T(8,128)} %param.9) | copy-start | bytes 1376260
  13.8 5.8 %copy-start.7 = (bf16[256,128]{1,0:T(8,128)(2,1)S(1)}, bf16[256,128]{1,0:T(8,128)(2,1)}, u32[]{:S(2)}) copy-start(bf16[256,128]{1,0:T(8,128)(2,1)} %constant.20.clone.table_ref) | copy-start | bytes 196612
  14.5 1.3 %copy-start.2 = (f32[4,64,1792]{2,1,0:T(8,128)}, f32[4,64,1792]{2,1,0:T(8,128)S(1)}, u32[]{:S(2)}) copy-start(f32[4,64,1792]{2,1,0:T(8,128)S(1)} %widen.1) | copy-start | bytes 5505028
  16.9 10.2 %collective-permute-start = (f32[4,64,1792]{2,1,0:T(8,128)}, f32[4,64,1792]{2,1,0:T(8,128)}, u32[]{:S(2)}, u32[]{:S(2)}) collective-permute-start(f32[4,64,1792]{2,1,0:T(8,128)} %copy-done.2), channel_id=1, source_target_pairs={{0,1},{1,0},{2,3},{3,2},{4,5},{5,4},{6,7},{7,6},{8,9},{9,8},{10,11... | collective-permute-start | bytes 5505032 | tf_op jit(solution)/shard_map/ppermute | solution.py:302
  23.9 8.0 %all-to-all-start.1 = ((f32[8,7,128]{2,1,0:T(8,128)}), f32[8,7,128]{2,1,0:T(8,128)S(1)}, u32[]{:S(2)}, u32[]{:S(2)}) async-start(f32[8,7,128]{2,1,0:T(8,128)} %get-tuple-element.20), calls=%async_computation.1 | async-start | bytes 65536 | tf_op jit(solution)/shard_map/all_to_all | solution.py:304
  28.9 0.8 %copy-start.4 = (f32[64,1792]{1,0:T(8,128)}, f32[64,1792]{1,0:T(8,128)S(1)}, u32[]{:S(2)}) copy-start(f32[64,1792]{1,0:T(8,128)S(1)} %get-tuple-element.31) | copy-start | bytes 1376260
  29.7 0.8 %copy-start.5 = (f32[64,1792]{1,0:T(8,128)}, f32[64,1792]{1,0:T(8,128)S(1)}, u32[]{:S(2)}) copy-start(f32[64,1792]{1,0:T(8,128)S(1)} %get-tuple-element.30) | copy-start | bytes 1376260
  30.4 29.8 %copy-start.6 = (bf16[512,256]{1,0:T(8,128)(2,1)S(1)}, bf16[512,256]{1,0:T(8,128)(2,1)}, u32[]{:S(2)}) copy-start(bf16[512,256]{1,0:T(8,128)(2,1)} %constant.22.clone.wide_ref) | copy-start | bytes 786436
  30.4 29.8 %copy-start.8 = (bf16[64,192]{1,0:T(8,128)(2,1)S(1)}, bf16[64,192]{1,0:T(8,128)(2,1)}, u32[]{:S(2)}) copy-start(bf16[64,192]{1,0:T(8,128)(2,1)} %constant.21.clone.tall_ref) | copy-start | bytes 73732
  32.6 22.5 %all-to-all-start.2 = ((f32[16,1,1792]{2,1,0:T(1,128)}), f32[16,1,1792]{2,1,0:T(1,128)S(1)}, u32[]{:S(2)}, u32[]{:S(2)}) async-start(f32[16,1,1792]{2,1,0:T(1,128)} %broadcast_in_dim.30), calls=%async_computation.2 | async-start | bytes 229376 | tf_op jit(solution)/shard_map/all_to_all | solution.py:290
  43.2 19.2 %collective-permute-start.1 = (f32[64,1792]{1,0:T(8,128)}, f32[64,1792]{1,0:T(8,128)S(1)}, u32[]{:S(2)}, u32[]{:S(2)}) collective-permute-start(f32[64,1792]{1,0:T(8,128)} %copy-done.5), channel_id=1, source_target_pairs={{0,4},{2,6},{4,0},{6,2},{1,5},{3,7},{5,1},{7,3},{8,12},{10,14},{12... | collective-permute-start | bytes 1376264 | tf_op jit(solution)/shard_map/ppermute | solution.py:312
  46.5 22.5 %collective-permute-start.2 = (f32[64,1792]{1,0:T(8,128)}, f32[64,1792]{1,0:T(8,128)S(1)}, u32[]{:S(2)}, u32[]{:S(2)}) collective-permute-start(f32[64,1792]{1,0:T(8,128)} %copy-done.4), channel_id=1, source_target_pairs={{0,2},{2,4},{4,6},{6,0},{1,3},{3,5},{5,7},{7,1},{8,10},{10,12},{12... | collective-permute-start | bytes 1376264 | tf_op jit(solution)/shard_map/ppermute | solution.py:312
  48.8 20.3 %collective-permute-start.3 = (f32[64,1792]{1,0:T(8,128)S(1)}, f32[64,1792]{1,0:T(8,128)}, u32[]{:S(2)}, u32[]{:S(2)}) collective-permute-start(f32[64,1792]{1,0:T(8,128)S(1)} %get-tuple-element.32), channel_id=1, source_target_pairs={{0,6},{2,0},{4,2},{6,4},{1,7},{3,1},{5,3},{7,5},{8,14},{10,8},{12,... | collective-permute-start | bytes 1376264 | tf_op jit(solution)/shard_map/ppermute | solution.py:312
  56.1 14.9 %all-to-all-start.3 = ((f32[4,1,28672]{2,1,0:T(1,128)}), f32[4,1,28672]{2,1,0:T(1,128)S(1)}, u32[]{:S(2)}, u32[]{:S(2)}) async-start(f32[4,1,28672]{2,1,0:T(1,128)} %broadcast_in_dim.34), calls=%async_computation.3 | async-start | bytes 917504 | tf_op jit(solution)/shard_map/all_to_all | solution.py:290
